TPU v7x, 256 devices: a whole 4x4x8 slice. The times are simulated.
256 devices in a mesh: elem: 32 (over z, x), plane: 8 (over y, core).
Axes of the slice: x: 4, y: 4, z: 8, core: 2. Of those that a mesh axis runs over, the one named last changes fastest.
Arguments:
- velocity: float32 [3, 128, 8, 8, 4096], P(None, 'plane', None, None, 'elem'), may hold values from -6 to 6
- elem_scale: float32 [2, 4096], P(None, 'elem'), may hold values from 0.6 to 1.6
- elem_ids: int32 [32, 128], P('elem'), may hold values from 0 to 4095, as said below
- edge_blocks: int32 [32, 2, 64], P('elem'), may hold values from 256 to 511, as said below
Outputs:
- velocity_new: float32 [3, 128, 8, 8, 4096], P(None, 'plane', None, None, 'elem')
- residual: float32 [3, 128, 8, 8, 4096], P(None, 'plane', None, None, 'elem')
Inputs may be any that keep to these rules, and one draw needn't show every extreme that they name: `elem_ids`: row d holds, in storage order, the ids of the 128 elements of radial rows 2d and 2d + 1; the element in radial row r at position j around has id r * 64 + j. edge_blocks[d, 0, j] is 256 plus the storage slot, within row d of elem_ids, of the element in radial row 2d at position j around; edge_blocks[d, 1, j] is 384 plus the storage slot of the element in radial row 2d + 1 at position j.
All inputs are finite; a program needn't handle non-finite values.
Results may differ from a plain program's by a relative error of at most 0.0009.
Values sent between devices are 32-bit elements; how exact they have to be, the bound alone decides.
A program may use at most 128 MiB of HBM per device.

v0:
```python
import math

import jax
import jax.numpy as jnp
import numpy as np
from jax import lax
from jax.sharding import PartitionSpec as P

ITERS = 2


penalty = 8.0
lam_zero = 4.0
wave_step = 0.1
highest = lax.Precision.HIGHEST


def passed_along(array, axis, by):
    count = lax.axis_size(axis)
    pairs = [(i, i + by) for i in range(count) if 0 <= i + by < count]
    return lax.ppermute(array, axis, pairs)


def node_tables(number):
    degree = number - 1
    points = -np.cos(np.pi * np.arange(number) / degree)
    scales = np.ones(number)
    scales[0] = 2.0
    scales[-1] = 2.0
    barycentric = (-1.0) ** np.arange(number) / scales
    derivative = np.zeros((number, number))
    for row_at in range(number):
        for col_at in range(number):
            if row_at != col_at:
                derivative[row_at, col_at] = (
                    barycentric[col_at] / barycentric[row_at] / (points[row_at] - points[col_at])
                )
        derivative[row_at, row_at] = -np.sum(derivative[row_at])
    weights = np.zeros(number)
    for node_at in range(number):
        running = 0.0
        for harmonic in range(1, degree // 2 + 1):
            factor = 2.0
            running += (
                factor
                / (4.0 * harmonic * harmonic - 1.0)
                * np.cos(2.0 * np.pi * node_at * harmonic / degree)
            )
        end_factor = 1.0 if node_at in (0, degree) else 2.0
        weights[node_at] = end_factor / degree * (1.0 - running)
    stiffness = derivative.T @ (weights[:, None] * derivative)
    return (
        jnp.asarray(derivative, jnp.float32),
        jnp.asarray(weights, jnp.float32),
        jnp.asarray(stiffness, jnp.float32),
    )


def mode_table(planes):
    mode_slots = jnp.arange(planes, dtype=jnp.int32)
    harmonic = mode_slots // 2
    phase_index = harmonic[:, None] * mode_slots[None, :] % planes
    angles = 2.0 * math.pi / planes * phase_index.astype(jnp.float32)
    cosine = jnp.cos(angles) * (2.0 / planes)
    sine_rows = jnp.sin(angles) * (2.0 / planes)
    fourier = jnp.where((mode_slots % 2 == 0)[:, None], cosine, sine_rows)
    mean_row = jnp.ones((planes,), jnp.float32) / planes
    alternating = jnp.where(mode_slots % 2 == 0, 1.0, -1.0).astype(jnp.float32) / planes
    return fourier.at[0].set(mean_row).at[1].set(alternating)


def element_geometry(members, scale_pair, circle, radial):
    row_index = (members // circle).astype(jnp.float32)
    growth = 1.0 + 2.0 * row_index / (radial - 1)
    return (scale_pair[0] * growth, scale_pair[1])


def neighbour_table(members, circle):
    row_index = members // circle
    beside_all = members % circle
    targets = jnp.stack(
        [
            row_index * circle + (beside_all - 1) % circle,
            row_index * circle + (beside_all + 1) % circle,
            members - circle,
            members + circle,
        ]
    )
    return (targets[:, :, None] == members[None, None, :]).astype(jnp.float32)


def with_products(velocity):
    return jnp.stack(
        [
            velocity[0],
            velocity[1],
            velocity[2],
            velocity[0] * velocity[0],
            velocity[0] * velocity[1],
            velocity[0] * velocity[2],
            velocity[1] * velocity[1],
            velocity[1] * velocity[2],
            velocity[2] * velocity[2],
        ]
    )


def edge_values(values):
    traces = jnp.stack(
        [values[:, 0, :, :], values[:, -1, :, :], values[:, :, 0, :], values[:, :, -1, :]], axis=2
    )
    return traces.reshape(values.shape[0] * values.shape[1], 4 * values.shape[3])


def helmholtz(
    values,
    rim_values,
    helm_shift,
    circ_size,
    radial_size,
    linkage,
    blocks,
    from_below,
    from_above,
    weights,
    stiffness,
):
    systems = values.shape[0]
    number = values.shape[1]
    elements = values.shape[3]
    sides = rim_values.reshape(systems * number, 4, elements)
    swapped = jnp.stack([sides[:, 1], sides[:, 0], sides[:, 3], sides[:, 2]], axis=1)
    facing = jnp.einsum("kst,sat->ksa", swapped, linkage, precision=highest)
    facing = facing.reshape(systems * number, 4 * elements)
    facing = facing.at[:, blocks[0]].add(from_below).at[:, blocks[1]].add(from_above)
    mismatch = (rim_values - facing).reshape(systems, number, 4, elements)
    coupling = penalty * weights[None, :, None, None] * mismatch
    mass_diag = (weights[:, None] * weights[None, :])[None, :, :, None] * (circ_size * radial_size)[
        None, None, None, :
    ]
    result = helm_shift[:, None, None, None] * mass_diag * values
    result = result + (radial_size / circ_size)[None, None, None, :] * weights[
        None, None, :, None
    ] * jnp.einsum("ac,kcbe->kabe", stiffness, values, precision=highest)
    result = result + (circ_size / radial_size)[None, None, None, :] * weights[
        None, :, None, None
    ] * jnp.einsum("bc,kace->kabe", stiffness, values, precision=highest)
    result = result.at[:, 0, :, :].add(coupling[:, :, 0]).at[:, -1, :, :].add(coupling[:, :, 1])
    result = result.at[:, :, 0, :].add(coupling[:, :, 2]).at[:, :, -1, :].add(coupling[:, :, 3])
    return result


def right_side(modal, circ_size, radial_size, pair_waves, derivative, weights):
    flux_index = ((3, 4, 5), (4, 6, 7), (5, 7, 8))
    modes = modal.shape[1]
    mass_diag = (weights[:, None] * weights[None, :])[:, :, None] * (circ_size * radial_size)[
        None, None, :
    ]
    components = []
    for component in range(3):
        flux_x = modal[flux_index[component][0]]
        flux_y = modal[flux_index[component][1]]
        flux_z = modal[flux_index[component][2]].reshape((modes // 2, 2) + modal.shape[2:])
        grad_x = jnp.einsum("ac,mcbe->mabe", derivative, flux_x, precision=highest) / circ_size
        grad_y = jnp.einsum("bc,mace->mabe", derivative, flux_y, precision=highest) / radial_size
        grad_z = (
            jnp.stack([flux_z[:, 1], -flux_z[:, 0]], axis=1)
            * (wave_step * pair_waves)[:, None, None, None, None]
        )
        advect = grad_x + grad_y + grad_z.reshape(modal.shape[1:])
        components.append(mass_diag[None] * (lam_zero * modal[component] - advect))
    return jnp.stack(components)


def inner_dot(first_vec, second_vec):
    return jnp.sum(first_vec * second_vec, axis=(1, 2, 3))


def squares(residual):
    return lax.psum(inner_dot(residual, residual), "elem")


def on_device(velocity, elem_scale, elem_ids, edge_blocks):
    number = velocity.shape[2]
    elements = velocity.shape[4]
    local_planes = velocity.shape[1]
    planes = local_planes * lax.axis_size("plane")
    derivative, weights, stiffness = node_tables(number)
    fourier = mode_table(planes)
    circle = elements // 2
    radial = 2 * lax.axis_size("elem")
    members = elem_ids[0]
    blocks = edge_blocks[0]
    circ_size, radial_size = element_geometry(members, elem_scale, circle, radial)
    linkage = neighbour_table(members, circle)
    first_slot = lax.axis_index("plane") * local_planes
    mode_slots = first_slot + jnp.arange(local_planes, dtype=jnp.int32)
    wavenumber = jnp.where(mode_slots == 1, planes // 2, mode_slots // 2).astype(jnp.float32)
    pair_waves = (first_slot // 2 + jnp.arange(local_planes // 2, dtype=jnp.int32)).astype(
        jnp.float32
    )
    fields = with_products(
        lax.all_to_all(velocity, "plane", split_axis=2, concat_axis=1, tiled=True)
    )
    spectral = jnp.einsum("mz,fzabe->fmabe", fourier, fields, precision=highest)
    modal = lax.all_to_all(spectral, "plane", split_axis=1, concat_axis=2, tiled=True)
    forcing = right_side(modal, circ_size, radial_size, pair_waves, derivative, weights)
    forcing = forcing.reshape(3 * local_planes, number, number, elements)
    helm_shift = jnp.tile(lam_zero + (wave_step * wavenumber) ** 2, 3)
    solution = jnp.zeros_like(forcing)
    residual = forcing
    direction = forcing
    norm_now = squares(residual)
    for sweep in range(ITERS):
        rim_values = edge_values(direction)
        from_below = passed_along(rim_values[:, blocks[1]], "elem", 1)
        from_above = passed_along(rim_values[:, blocks[0]], "elem", -1)
        applied = helmholtz(
            direction,
            rim_values,
            helm_shift,
            circ_size,
            radial_size,
            linkage,
            blocks,
            from_below,
            from_above,
            weights,
            stiffness,
        )
        step_len = norm_now / lax.psum(inner_dot(direction, applied), "elem")
        solution = solution + step_len[:, None, None, None] * direction
        residual = residual - step_len[:, None, None, None] * applied
        norm_next = squares(residual)
        direction = residual + (norm_next / norm_now)[:, None, None, None] * direction
        norm_now = norm_next
    shape_out = (3, local_planes, number, number, elements)
    return (solution.reshape(shape_out), residual.reshape(shape_out))


def solution(mesh):
    in_specs = (
        P(None, "plane", None, None, "elem"),
        P(None, "elem"),
        P("elem", None),
        P("elem", None, None),
    )
    out_specs = (P(None, "plane", None, None, "elem"), P(None, "plane", None, None, "elem"))
    return jax.shard_map(
        on_device, mesh=mesh, in_specs=in_specs, out_specs=out_specs, check_vma=False
    )
```

profile of v0, /device:TPU:2, one launch (start us, length us, event | category | flops | bytes accessed | tf_op | source)
XLA Modules:
  0.0 448.1 jit_solution(18419386127462434096)
XLA Ops:
  0.6 2.7 copy.83
  3.4 4.5 all-to-all-start
  8.3 21.1 %all-to-all-done = f32[3,16,8,8,128]{4,3,1,0,2:T(8,128)S(1)} async-done(((f32[3,16,8,8,128]{4,3,1,0,2:T(8,128)}), f32[3,16,8,8,128]{4,3,1,0,2:T(8,128)S(1)}, u32[]{:S(2)}, u32[]{:S(2)}) %all-to-all-start) | async-done | bytes 1572896 | tf_op jit(solution)/shard_map/all_to_all | solution.py:203
  38.0 7.1 %fusion.2 = f32[9,128,1,8,128]{1,4,3,0,2:T(8,128)} fusion(f32[9,128,1,8,128]{1,4,3,0,2:T(8,128)} %multiply_dynamic-update-slice_fusion, f32[128,128]{1,0:T(8,128)S(1)} %scatter.9), kind=kOutput, calls=%fused_computation.11 | convolution fusion | flops 1811939328 | bytes 9502720 | tf_op jit(solution)/shard_map/mz,fzabe->fmabe/dot_general | solution.py:205
  45.1 6.1 %copy.100 = f32[9,128,1,8,128]{4,3,0,2,1:T(8,128)} copy(f32[9,128,1,8,128]{1,4,3,0,2:T(8,128)} %fusion.2) | data formatting | bytes 9437184 | tf_op jit(solution)/shard_map/mz,fzabe->fmabe/transpose | solution.py:205
  51.2 4.9 %all-to-all-start.1 = ((f32[9,128,1,8,128]{4,3,0,2,1:T(8,128)}), f32[9,128,1,8,128]{4,3,0,2,1:T(8,128)}, u32[]{:S(2)}, u32[]{:S(2)}) async-start(f32[9,128,1,8,128]{4,3,0,2,1:T(8,128)} %copy.100), calls=%async_computation.1 | async-start | bytes 9437184 | tf_op jit(solution)/shard_map/all_to_all | solution.py:206
  57.9 53.4 %all-to-all-done.1 = f32[9,128,1,8,128]{4,3,0,2,1:T(8,128)} async-done(((f32[9,128,1,8,128]{4,3,0,2,1:T(8,128)}), f32[9,128,1,8,128]{4,3,0,2,1:T(8,128)}, u32[]{:S(2)}, u32[]{:S(2)}) %all-to-all-start.1) | async-done | bytes 4718624 | tf_op jit(solution)/shard_map/all_to_all | solution.py:206
  111.3 5.1 %copy.173 = f32[9,8,16,1,8,128]{5,1,4,2,3,0:T(8,128)S(1)} copy(f32[9,8,16,1,8,128]{5,4,0,2,1,3:T(8,128)} %bitcast.14) | data formatting | bytes 9437184 | tf_op jit(solution)/shard_map/all_to_all | solution.py:206
  125.7 3.4 collective-permute-start
  130.6 3.4 collective-permute-start.1
  140.3 3.3 scatter_custom_fusion
  143.6 3.3 scatter_custom_fusion.1
  153.9 3.9 scatter-add.56
  158.9 3.9 scatter-add.59
  165.4 73.1 %all-reduce = (f32[48]{0:T(128)S(1)}, f32[48]{0:T(128)S(1)}) all-reduce(f32[48]{0:T(128)S(1)} %copy-done.32, f32[48]{0:T(128)S(1)} %multiply_reduce_fusion.2), channel_id=1, replica_groups=mesh['elem'=32,'plane'=8] {'elem'}, use_global_device_ids=true, to_apply=%region_1.2 | all-reduce | flops 96 | bytes 768 | tf_op jit(solution)/shard_map/psum | solution.py:180
  239.2 74.5 %psum.30 = f32[48]{0:T(128)S(1)} all-reduce(f32[48]{0:T(128)S(1)} %multiply_reduce_fusion.1), channel_id=1, replica_groups=mesh['elem'=32,'plane'=8] {'elem'}, use_global_device_ids=true, to_apply=%region_7.8 | all-reduce | flops 48 | bytes 384 | tf_op jit(solution)/shard_map/psum | solution.py:180
  324.1 3.1 fusion.9
  329.2 4.3 collective-permute-start.3
  333.6 3.0 fusion.8
  338.8 3.3 scatter_custom_fusion.2
  342.2 3.3 scatter_custom_fusion.3
  354.1 6.1 %scatter-add.76 = f32[48,8,8,128]{3,1,2,0:T(8,128)} dynamic-update-slice(f32[48,8,8,128]{3,1,2,0:T(8,128)} %fusion.8, f32[48,1,8,128]{3,1,2,0:T(1,128)S(1)} %slice_add_fusion.3, s32[]{:T(128)} %constant.368.clone.1, s32[]{:T(128)} %constant.368.clone.1, s32[]{:T(128)} %constant.368.clone.1, s32[]{:T(128)} %constant.368.clone.1) | dynamic-update-slice | bytes 393220 | tf_op jit(solution)/shard_map/scatter-add | solution.py:148
  361.8 6.1 %scatter-add.77 = f32[48,8,8,128]{3,1,2,0:T(8,128)} dynamic-update-slice(f32[48,8,8,128]{3,1,2,0:T(8,128)} %scatter-add.76, f32[48,1,8,128]{3,1,2,0:T(1,128)S(1)} %slice_add_fusion.2, s32[]{:T(128)} %constant.368.clone.1, s32[]{:T(128)} %constant.390.clone.1, s32[]{:T(128)} %constant.368.clone.1, s32[]{:T(128)} %constant.368.clone.1) | dynamic-update-slice | bytes 393220 | tf_op jit(solution)/shard_map/scatter-add | solution.py:148
  373.7 69.0 %psum.31 = f32[48]{0:T(128)S(1)} all-reduce(f32[48]{0:T(128)S(1)} %multiply_reduce_fusion), channel_id=1, replica_groups=mesh['elem'=32,'plane'=8] {'elem'}, use_global_device_ids=true, to_apply=%region_11.12 | all-reduce | flops 48 | bytes 384 | tf_op jit(solution)/shard_map/psum | solution.py:231
  (172 shorter events, 74.9 us)
Async XLA Ops:
  3.4 26.1 %all-to-all-start = ((f32[3,16,8,8,128]{4,3,1,0,2:T(8,128)}), f32[3,16,8,8,128]{4,3,1,0,2:T(8,128)S(1)}, u32[]{:S(2)}, u32[]{:S(2)}) async-start(f32[3,16,8,8,128]{4,3,1,0,2:T(8,128)} %copy.83), calls=%async_computation | async-start | bytes 3145728 | tf_op jit(solution)/shard_map/all_to_all | solution.py:203
  51.2 5.7 %copy-start.18 = (s32[1,128]{1,0:T(1,128)S(1)}, s32[1,128]{1,0:T(1,128)}, u32[]{:S(2)}) copy-start(s32[1,128]{1,0:T(1,128)} %param.29) | copy-start | bytes 1540
  51.2 5.8 %copy-start.31 = (s32[1,2,64]{2,1,0:T(2,128)S(1)}, s32[1,2,64]{2,1,0:T(2,128)}, u32[]{:S(2)}) copy-start(s32[1,2,64]{2,1,0:T(2,128)} %param.30) | copy-start | bytes 1540
  51.2 6.4 %copy-start.26 = (f32[2,128]{1,0:T(2,128)S(1)}, f32[2,128]{1,0:T(2,128)}, u32[]{:S(2)}) copy-start(f32[2,128]{1,0:T(2,128)} %param.28) | copy-start | bytes 3076
  51.2 6.5 %copy-start.25 = (f32[8]{0:T(128)S(1)}, f32[8]{0:T(128)}, u32[]{:S(2)}) copy-start(f32[8]{0:T(128)} %constant.392.clone) | copy-start | bytes 100
  51.2 60.0 %all-to-all-start.1 = ((f32[9,128,1,8,128]{4,3,0,2,1:T(8,128)}), f32[9,128,1,8,128]{4,3,0,2,1:T(8,128)}, u32[]{:S(2)}, u32[]{:S(2)}) async-start(f32[9,128,1,8,128]{4,3,0,2,1:T(8,128)} %copy.100), calls=%async_computation.1 | async-start | bytes 9437184 | tf_op jit(solution)/shard_map/all_to_all | solution.py:206
  57.9 63.2 %copy-start.12 = (f32[8,8,128]{2,0,1:T(8,128)}, f32[8,8,128]{2,0,1:T(8,128)S(1)}, u32[]{:S(2)}) copy-start(f32[8,8,128]{2,0,1:T(8,128)S(1)} %broadcast_multiply_fusion) | copy-start | bytes 98308
  124.2 6.4 %copy-start.4 = (f32[384,512]{0,1:T(8,128)}, f32[384,512]{0,1:T(8,128)S(1)}, u32[]{:S(2)}) copy-start(f32[384,512]{0,1:T(8,128)S(1)} %copy.116) | copy-start | bytes 2359300
  124.2 9.8 %copy-start.16 = (f32[8,8,1,1]{1,0,3,2:T(8,128)S(1)}, f32[8,8,1,1]{1,0,3,2:T(8,128)}, u32[]{:S(2)}) copy-start(f32[8,8,1,1]{1,0,3,2:T(8,128)} %constant.398) | copy-start | bytes 772
  125.7 14.6 %collective-permute-start = (f32[384,64]{0,1:T(8,128)}, f32[384,64]{0,1:T(8,128)}, u32[]{:S(2)}, u32[]{:S(2)}) collective-permute-start(f32[384,64]{0,1:T(8,128)} %bitcast.61), channel_id=1, source_target_pairs={{0,8},{8,16},{16,24},{24,32},{32,40},{40,48},{48,56},{56,64},{64,7... | collective-permute-start | bytes 294920 | tf_op jit(solution)/shard_map/ppermute | solution.py:21
  130.6 5.0 %copy-start.23 = (f32[48]{0:T(128)S(1)}, f32[48]{0:T(128)}, u32[]{:S(2)}) copy-start(f32[48]{0:T(128)} %mul.523) | copy-start | bytes 580
  130.6 13.1 %collective-permute-start.1 = (f32[384,64]{0,1:T(8,128)}, f32[384,64]{0,1:T(8,128)}, u32[]{:S(2)}, u32[]{:S(2)}) collective-permute-start(f32[384,64]{0,1:T(8,128)} %bitcast.63), channel_id=1, source_target_pairs={{8,0},{16,8},{24,16},{32,24},{40,32},{48,40},{56,48},{64,56},{72,6... | collective-permute-start | bytes 294920 | tf_op jit(solution)/shard_map/ppermute | solution.py:21
  137.5 9.5 %copy-start = (f32[48,8,8,128]{3,1,2,0:T(8,128)}, f32[48,8,8,128]{3,1,2,0:T(8,128)S(1)}, u32[]{:S(2)}) copy-start(f32[48,8,8,128]{3,1,2,0:T(8,128)S(1)} %fusion.6) | copy-start | bytes 4718596
  238.4 75.3 %copy-start.21 = (f32[48]{0:T(128)}, f32[48]{0:T(128)S(1)}, u32[]{:S(2)}) copy-start(f32[48]{0:T(128)S(1)} %div.172) | copy-start | bytes 580
  324.1 9.4 %copy-start.3 = (f32[48,8,8,128]{3,1,2,0:T(8,128)S(1)}, f32[48,8,8,128]{3,1,2,0:T(8,128)}, u32[]{:S(2)}) copy-start(f32[48,8,8,128]{3,1,2,0:T(8,128)} %copy-done.2) | copy-start | bytes 4718596
  324.1 9.4 %copy-start.14 = (f32[8,8,128]{2,0,1:T(8,128)S(1)}, f32[8,8,128]{2,0,1:T(8,128)}, u32[]{:S(2)}) copy-start(f32[8,8,128]{2,0,1:T(8,128)} %copy-done.12) | copy-start | bytes 98308
  324.1 9.5 %copy-start.24 = (f32[48]{0:T(128)S(1)}, f32[48]{0:T(128)}, u32[]{:S(2)}) copy-start(f32[48]{0:T(128)} %mul.523) | copy-start | bytes 580
  327.3 10.9 %collective-permute-start.2 = (f32[384,64]{0,1:T(8,128)S(1)}, f32[384,64]{0,1:T(8,128)S(1)}, u32[]{:S(2)}, u32[]{:S(2)}) collective-permute-start(f32[384,64]{0,1:T(8,128)S(1)} %bitcast.278), channel_id=1, source_target_pairs={{0,8},{8,16},{16,24},{24,32},{32,40},{40,48},{48,56},{56,64},{64,7... | collective-permute-start | bytes 294920 | tf_op jit(solution)/shard_map/ppermute | solution.py:21
  329.2 7.4 %copy-start.7 = (f32[384,1,128]{2,0,1:T(8,128)S(1)}, f32[384,1,128]{2,0,1:T(8,128)}, u32[]{:S(2)}) copy-start(f32[384,1,128]{2,0,1:T(8,128)} %get-tuple-element.143) | copy-start | bytes 589828
  329.2 7.4 %copy-start.8 = (f32[384,1,128]{2,0,1:T(8,128)S(1)}, f32[384,1,128]{2,0,1:T(8,128)}, u32[]{:S(2)}) copy-start(f32[384,1,128]{2,0,1:T(8,128)} %get-tuple-element.144) | copy-start | bytes 589828
  329.2 7.4 %copy-start.20 = (s32[1,128]{1,0:T(1,128)S(1)}, s32[1,128]{1,0:T(1,128)}, u32[]{:S(2)}) copy-start(s32[1,128]{1,0:T(1,128)} %param.29) | copy-start | bytes 1540
  329.2 12.9 %collective-permute-start.3 = (f32[384,64]{0,1:T(8,128)}, f32[384,64]{0,1:T(8,128)}, u32[]{:S(2)}, u32[]{:S(2)}) collective-permute-start(f32[384,64]{0,1:T(8,128)} %bitcast.83), channel_id=1, source_target_pairs={{8,0},{16,8},{24,16},{32,24},{40,32},{48,40},{56,48},{64,56},{72,6... | collective-permute-start | bytes 294920 | tf_op jit(solution)/shard_map/ppermute | solution.py:21
  371.4 71.3 %copy-start.34 = (f32[48]{0:T(128)S(1)}, f32[48]{0:T(128)}, u32[]{:S(2)}) copy-start(f32[48]{0:T(128)} %copy-done.33) | copy-start | bytes 580
  371.4 71.3 %copy-start.22 = (f32[48]{0:T(128)S(1)}, f32[48]{0:T(128)}, u32[]{:S(2)}) copy-start(f32[48]{0:T(128)} %copy-done.21) | copy-start | bytes 580
  (18 other events, 38.6 us)
where the time goes:
time: 451 us; the launch traced here: 448 us
  blocking collectives  217 us (48%)
  waiting for transfers between devices  74.5 us (17%)
  local copies, waits for them, and re-layouts  64.1 us (14%)
  other arithmetic  45.4 us (10%)
  matrix products  23.8 us (5%)
  starting transfers between devices  22.4 us (5%)
    psum x2, blocking collectives, squares(): return lax.psum(inner_dot(residual, residual), 'elem')  148 us
    psum x1, blocking collectives, on_device(): step_len = norm_now / lax.psum(inner_dot(direction, applied), 'elem')  69 us
    all_to_all x1, waiting for transfers between devices, on_device(): lax.all_to_all(spectral, 'plane', split_axis=1, concat_axis=2, tiled=True)  53.4 us
    all_to_all x1, waiting for transfers between devices, on_device(): lax.all_to_all(velocity, 'plane', split_axis=2, concat_axis=1, tiled=True)  21.1 us
    scatter-add x4, local copies, waits for them, and re-layouts, helmholtz(): result.at[:, 0, :, :].add(coupling[:, :, 0]).at[:, -1, :, :]  19.9 us
    scatter-add x4, other arithmetic, helmholtz(): facing.at[:, blocks[0]].add(from_below).at[:, blocks[1]].add(from_above)  13.3 us
    ppermute x4, starting transfers between devices, passed_along(): return lax.ppermute(array, axis, pairs)  13 us
    unnamed x76, local copies, waits for them, and re-layouts  11.9 us
  transfers between devices with their start and end apart: 6, of which 2 were waited for; matrix products, arithmetic and copies ran while one was open for 5% of the time, Pallas kernels for 0%

commit v1 on v0

v1 whole, which is shorter than its diff:
```python
import functools
import math

import jax
import jax.numpy as jnp
import ml_dtypes
import numpy as np
from jax import lax
from jax.experimental import pallas as pl
from jax.experimental.pallas import tpu as pltpu
from jax.sharding import PartitionSpec as P

MESH = pl.DeviceIdType.MESH
F32 = jnp.float32
BF16 = jnp.bfloat16

N = 8
ED = 128
Z = 128
NP = 8
ZL = Z // NP
EG = ED // NP
SYS = 3 * ZL
NX = 4
NZ = 8
NE = NX * NZ
PEN = 8.0
LAM = 4.0
STEP = 0.1


def node_tables():
    degree = N - 1
    points = -np.cos(np.pi * np.arange(N) / degree)
    scales = np.ones(N)
    scales[0] = 2.0
    scales[-1] = 2.0
    bary = (-1.0) ** np.arange(N) / scales
    deriv = np.zeros((N, N))
    for i in range(N):
        for j in range(N):
            if i != j:
                deriv[i, j] = bary[j] / bary[i] / (points[i] - points[j])
        deriv[i, i] = -np.sum(deriv[i])
    weights = np.zeros(N)
    for i in range(N):
        running = 0.0
        for k in range(1, degree // 2 + 1):
            factor = 1.0 if 2 * k == degree else 2.0
            running += factor / (4.0 * k * k - 1.0) * np.cos(2.0 * np.pi * i * k / degree)
        weights[i] = (1.0 if i in (0, degree) else 2.0) / degree * (1.0 - running)
    stiff = deriv.T @ (weights[:, None] * deriv)
    return deriv, weights, stiff


def mode_matrix():
    slots = np.arange(Z)
    harmonic = slots // 2
    angles = 2.0 * math.pi / Z * (harmonic[:, None] * slots[None, :] % Z)
    four = np.where((slots % 2 == 0)[:, None], np.cos(angles), np.sin(angles)) * (2.0 / Z)
    four[0] = 1.0 / Z
    four[1] = np.where(slots % 2 == 0, 1.0, -1.0) / Z
    dz = np.zeros((Z, Z))
    wave = STEP * np.arange(Z // 2)
    dz[0::2] = wave[:, None] * four[1::2]
    dz[1::2] = -wave[:, None] * four[0::2]
    return np.concatenate([four, -dz], axis=1)


def halves(table):
    high = table.astype(np.float32).astype(ml_dtypes.bfloat16)
    low = (table - high.astype(np.float64)).astype(np.float32).astype(ml_dtypes.bfloat16)
    return np.stack([high, low])


DERIV, WEIGHTS, STIFF = node_tables()


def split(x):
    high = x.astype(BF16)
    return high, (x - high.astype(F32)).astype(BF16)


def dot(x, y):
    return jnp.dot(x, y, preferred_element_type=F32)


def pick(x, table):
    high, low = split(x)
    return dot(high, table) + dot(low, table)


def block_transpose(rows):
    rows = list(rows)
    lane = lax.broadcasted_iota(jnp.int32, rows[0].shape, rows[0].ndim - 1) // EG
    for d in (1, 2, 4):
        clear = (lane & d) == 0
        for i in range(NP):
            if i & d == 0:
                x, y = rows[i], rows[i + d]
                axis = x.ndim - 1
                rows[i] = jnp.where(clear, x, pltpu.roll(y, EG * d, axis))
                rows[i + d] = jnp.where(clear, pltpu.roll(x, ED - EG * d, axis), y)
    return rows


def stiff_times(v):
    even = [v[p] + v[N - 1 - p] for p in range(N // 2)]
    odd = [v[p] - v[N - 1 - p] for p in range(N // 2)]
    out = [None] * N
    for a in range(N // 2):
        s = [0.5 * (STIFF[a, p] + STIFF[a, N - 1 - p]) for p in range(N // 2)]
        t = [0.5 * (STIFF[a, p] - STIFF[a, N - 1 - p]) for p in range(N // 2)]
        e = sum(float(s[p]) * even[p] for p in range(1, N // 2)) + float(s[0]) * even[0]
        o = sum(float(t[p]) * odd[p] for p in range(1, N // 2)) + float(t[0]) * odd[0]
        out[a] = e + o
        out[N - 1 - a] = e - o
    return out


def kernel(
    vel,
    scale,
    ids,
    wlane,
    fmat,
    dkron,
    dtab,
    r_out,
    q_out,
    p_out,
    coef_out,
    vin,
    xsend,
    xbuf,
    acc,
    bbuf,
    fsend,
    fbuf,
    res,
    qv,
    pv,
    geo,
    hel,
    tables,
    face,
    edge,
    hsend,
    hrecv,
    dots,
    rbuf1,
    rbuf2,
    in_sem,
    out_sem,
    s1,
    r1,
    s2,
    r2,
    hs,
    hr,
    as1,
    ar1,
    as2,
    ar2,
):
    e = lax.axis_index("elem")
    me = lax.axis_index("plane")
    y, core = me // 2, lax.rem(me, 2)
    z, x = e // NX, lax.rem(e, NX)
    plane_offsets = [(dy, dc) for dy in (2, 1, 3, 0) for dc in (0, 1) if (dy, dc) != (0, 0)]
    plane_peers = [lax.rem(y + dy, 4) * 2 + lax.rem(core + dc, 2) for dy, dc in plane_offsets]
    x_peers = [z * NX + lax.rem(x + d, NX) for d in (2, 1, 3)]
    z_peers = [lax.rem(z + d, NZ) * NX + x for d in (4, 3, 5, 2, 6, 1, 7)]
    up, down = lax.rem(e + 1, NE), lax.rem(e + NE - 1, NE)

    load = pltpu.make_async_copy(vel, vin, in_sem)
    load.start()
    barrier = pltpu.get_barrier_semaphore()
    for t in plane_peers:
        pl.semaphore_signal(barrier, inc=1, device_id=(e, t), device_id_type=MESH)
    for t in x_peers + z_peers + [up, down]:
        pl.semaphore_signal(barrier, inc=1, device_id=(t, me), device_id_type=MESH)

    lid = ids[...] & (ED - 1)
    growth = 1.0 + 2.0 * (ids[...] // 64).astype(F32) / 63.0
    circ = scale[0:1, :] * growth
    radial = scale[1:2, :]
    geo[0:1, :] = circ * radial
    geo[1:2, :] = radial / circ
    geo[2:3, :] = circ / radial
    lane_row = lax.broadcasted_iota(jnp.int32, (1, ED), 1)
    for k, val in ((3, circ), (4, radial)):
        val = pltpu.roll(jnp.broadcast_to(val, (8, ED)), lax.rem(ED - EG * me, ED), 1)
        val = jnp.where(lax.broadcasted_iota(jnp.int32, (8, ED), 1) < EG, val, 0.0)
        for d in (1, 2, 4):
            val = val + pltpu.roll(val, EG * d, 1)
        geo[k : k + 1, :] = val[0:1, :]
    wl = wlane[...]
    g_circ, g_radial = geo[3:4, :], geo[4:5, :]
    geo[5:6, :] = g_circ * g_radial * wl
    geo[6:7, :] = g_circ * wl
    geo[7:8, :] = g_radial * wl
    load.wait()
    pl.semaphore_wait(barrier, NP - 1 + 3 + 7 + 2)

    def copy1(a, i):
        t = plane_peers[i]
        return pltpu.make_async_remote_copy(
            src_ref=xsend.at[a, t],
            dst_ref=xbuf.at[a, :, pl.ds(pl.multiple_of(me * ZL, ZL), ZL), :],
            send_sem=s1.at[a, i],
            recv_sem=r1.at[a, i],
            device_id=(e, t),
            device_id_type=MESH,
        )

    def copy2(a, i):
        t = plane_peers[i]
        return pltpu.make_async_remote_copy(
            src_ref=fsend.at[a, :, pl.ds(pl.multiple_of(t * ZL, ZL), ZL), :],
            dst_ref=fbuf.at[a, me],
            send_sem=s2.at[a, i],
            recv_sem=r2.at[a, i],
            device_id=(e, t),
            device_id_type=MESH,
        )

    def send_first(a, carry):
        for c in range(3):
            for h in range(ZL // 8):
                base = (c * ZL + h * 8) * N * N + a * N
                rows = [vin[pl.ds(base + b, 8, stride=N * N), :] for b in range(N)]
                for q, row in enumerate(block_transpose(rows)):
                    xsend[a, q, c, pl.ds(h * 8, 8), :] = row
        for i in range(NP - 1):
            copy1(a, i).start()
        mine = pl.ds(pl.multiple_of(me * ZL, ZL), ZL)
        xbuf[a, :, mine, :] = xsend[a, me]
        return carry

    lax.fori_loop(0, N, send_first, 0)

    acc[...] = jnp.zeros_like(acc)
    dots[...] = jnp.zeros_like(dots)
    row_i = lax.broadcasted_iota(jnp.int32, (ED, ED), 0)
    lane_i = lax.broadcasted_iota(jnp.int32, (ED, ED), 1)
    lid_l = jnp.broadcast_to(lid, (ED, ED))
    lid_t = jnp.transpose(lid_l.astype(F32)).astype(jnp.int32)

    def ones(where):
        return jnp.where(where, 1.0, 0.0).astype(BF16)

    tables[0] = ones(lid_t == ((lid_l & 64) | ((lid_l + 63) & 63)))
    tables[1] = ones(lid_t == ((lid_l & 64) | ((lid_l + 1) & 63)))
    tables[2] = ones((lid_t == (lid_l ^ 64)) & (lid_l >= 64))
    tables[3] = ones((lid_t == (lid_l ^ 64)) & (lid_l < 64))
    tables[4] = ones(lid_t == lane_i + 64)
    tables[5] = ones((lid_t == lane_i) & (lane_i >= 64))
    tables[6] = ones((lid_t == lane_i) & (lane_i < 64))
    tables[7] = ones(lid_t + 64 == lane_i)
    tables[8] = ones((row_i == lid_l) & (lid_l < 64))
    tables[9] = ones(row_i == lid_l + 64)
    tables[10] = ones(row_i + 64 == lid_l)
    tables[11] = ones((row_i == lid_l) & (lid_l >= 64))
    slot = me * ZL + (lax.broadcasted_iota(jnp.int32, (SYS, ED), 0) & (ZL - 1))
    kappa = jnp.where(slot == 1, Z // 2, slot // 2).astype(F32)
    hel[...] = (LAM + (STEP * kappa) * (STEP * kappa)) * geo[0:1, :]

    def arrive_first(p, carry):
        for i in range(NP - 1):
            copy1(p, i).wait_recv()
        w_p = dtab[N, p]
        mass = geo[5:6, :] * w_p
        g_y = geo[6:7, :] * w_p
        g_x = geo[7:8, :]
        for c in range(3):
            fy_high, fy_low = split(xbuf[p, 1] * xbuf[p, c])
            dy = dot(fy_high, dkron[0]) + dot(fy_low, dkron[0]) + dot(fy_high, dkron[1])
            acc[p, c] += (LAM * mass) * xbuf[p, c] - g_y * dy
            b_high, b_low = split(mass * (xbuf[p, 2] * xbuf[p, c]))
            bbuf[p, 0, c] = b_high
            bbuf[p, 1, c] = b_low
            for h in range(4):
                rows = pl.ds(h * 32, 32)
                fx = g_x * (xbuf[p, 0, rows, :] * xbuf[p, c, rows, :])
                for a in range(N):
                    acc[a, c, rows, :] += dtab[a, p] * fx
        return carry

    lax.fori_loop(0, N, arrive_first, 0)

    def send_second(a, carry):
        for c in range(3):
            a_high, a_low = split(acc[a, c])
            high = jnp.concatenate([a_high, bbuf[a, 0, c]], axis=0)
            low = jnp.concatenate([a_low, bbuf[a, 1, c]], axis=0)
            fsend[a, c] = dot(fmat[0], high) + dot(fmat[0], low) + dot(fmat[1], high)
        for i in range(NP - 1):
            copy2(a, i).start()
        fbuf[a, me] = fsend[a, :, pl.ds(pl.multiple_of(me * ZL, ZL), ZL), :]
        return carry

    lax.fori_loop(0, N, send_second, 0)

    def arrive_second(a, carry):
        for i in range(NP - 1):
            copy2(a, i).wait_recv()
        for c in range(3):
            for h in range(ZL // 8):
                rows = [fbuf[a, s, c, pl.ds(h * 8, 8), :] for s in range(NP)]
                for b, row in enumerate(block_transpose(rows)):
                    res[a * N + b, pl.ds(c * ZL + h * 8, 8), :] = row
        return carry

    lax.fori_loop(0, N, arrive_second, 0)
    r_copy = pltpu.make_async_copy(res, r_out, out_sem.at[0])
    r_copy.start()

    def halo(kind, way):
        return pltpu.make_async_remote_copy(
            src_ref=hsend.at[kind, way],
            dst_ref=hrecv.at[kind, way],
            send_sem=hs.at[kind, way],
            recv_sem=hr.at[kind, way],
            device_id=((up, down)[way], me),
            device_id_type=MESH,
        )

    def send_edges(v, kind):
        for a in range(N // 2):
            for way, b, t in ((0, N - 1, 4), (1, 0, 6)):
                hsend[kind, way, a] = pick(v[a * N + b], tables[t]) + pick(
                    v[(a + N // 2) * N + b], tables[t + 1]
                )
        halo(kind, 0).start()
        halo(kind, 1).start()

    def take_edges(kind):
        for way in (0, 1):
            halo(kind, way).wait_recv()
            there = (e > 0) if way == 0 else (e < NE - 1)
            for half in (0, 1):
                got = hrecv[kind, way].reshape(N // 2 * SYS, ED)
                got = pick(got, tables[8 + 2 * way + half])
                got = jnp.where(there, got, 0.0)
                edge[way, pl.ds(half * (N // 2), N // 2)] = got.reshape(N // 2, SYS, ED)

    def apply_local(v, q):
        face[0] = pick(v[(N - 1) * N : N * N].reshape(N * SYS, ED), tables[0]).reshape(N, SYS, ED)
        face[1] = pick(v[0:N].reshape(N * SYS, ED), tables[1]).reshape(N, SYS, ED)
        for a in range(N):
            face[2, a] = pick(v[a * N + N - 1], tables[2])
            face[3, a] = pick(v[a * N], tables[3])

        def tile(st, carry):
            rows = pl.ds(pl.multiple_of(st * 8, 8), 8)
            hm = hel[rows, :]
            kx = jnp.broadcast_to(geo[1:2, :], (8, ED))
            ky = jnp.broadcast_to(geo[2:3, :], (8, ED))
            for b in range(N):
                col = stiff_times([v[a * N + b, rows, :] for a in range(N)])
                scale_b = kx * float(WEIGHTS[b])
                for a in range(N):
                    q[a * N + b, rows, :] = scale_b * col[a]
            for a in range(N):
                vals = [v[a * N + b, rows, :] for b in range(N)]
                line = stiff_times(vals)
                scale_a = ky * float(WEIGHTS[a])
                hm_a = hm * float(WEIGHTS[a])
                for b in range(N):
                    out = q[a * N + b, rows, :] + scale_a * line[b]
                    out = out + (hm_a * float(WEIGHTS[b])) * vals[b]
                    if a == 0:
                        out = out + float(PEN * WEIGHTS[b]) * (vals[b] - face[0, b, rows, :])
                    if a == N - 1:
                        out = out + float(PEN * WEIGHTS[b]) * (vals[b] - face[1, b, rows, :])
                    if b == 0:
                        out = out + float(PEN * WEIGHTS[a]) * (vals[b] - face[2, a, rows, :])
                    if b == N - 1:
                        out = out + float(PEN * WEIGHTS[a]) * (vals[b] - face[3, a, rows, :])
                    q[a * N + b, rows, :] = out
            return carry

        lax.fori_loop(0, SYS // 8, tile, 0)

    def add_edges(q):
        for a in range(N):
            q[a * N] -= float(PEN * WEIGHTS[a]) * edge[0, a]
            q[a * N + N - 1] -= float(PEN * WEIGHTS[a]) * edge[1, a]

    send_edges(res, 0)
    apply_local(res, qv)
    send_edges(qv, 1)
    take_edges(0)
    add_edges(qv)
    q_copy = pltpu.make_async_copy(qv, q_out, out_sem.at[1])
    q_copy.start()
    apply_local(qv, pv)
    take_edges(1)
    inner = jnp.broadcast_to(lid < 64, (SYS, ED)) & (e > 0)
    outer = jnp.broadcast_to(lid >= 64, (SYS, ED)) & (e < NE - 1)
    for a in range(N):
        w_a = float(PEN * WEIGHTS[a])
        edge[0, a] -= jnp.where(inner, w_a * res[a * N], 0.0)
        edge[1, a] -= jnp.where(outer, w_a * res[a * N + N - 1], 0.0)
    add_edges(pv)
    p_copy = pltpu.make_async_copy(pv, p_out, out_sem.at[2])
    p_copy.start()

    def dot_tile(st, carry):
        rows = pl.ds(pl.multiple_of(st * 8, 8), 8)
        sums = [jnp.zeros((8, ED), F32) for _ in range(4)]
        for n in range(N * N):
            r_n, q_n, p_n = res[n, rows, :], qv[n, rows, :], pv[n, rows, :]
            for k, prod in enumerate((r_n * r_n, r_n * q_n, q_n * q_n, q_n * p_n)):
                sums[k] = sums[k] + prod
        for k in range(4):
            dots[k, rows, :] = sums[k]
        return carry

    lax.fori_loop(0, SYS // 8, dot_tile, 0)
    one_rows = jnp.ones((8, ED), F32)
    row8 = lax.broadcasted_iota(jnp.int32, (8, ED), 0)
    part = jnp.zeros((8, ED), F32)
    for k in range(4):
        summed = lax.dot_general(
            one_rows,
            dots[k],
            (((1,), (1,)), ((), ())),
            precision=lax.Precision.HIGHEST,
            preferred_element_type=F32,
        )
        part = jnp.where(row8 == k, summed, part)

    def reduce(value, buf, peers, send, recv):
        buf[0] = value
        copies = []
        for i, t in enumerate(peers):
            copies.append(
                pltpu.make_async_remote_copy(
                    src_ref=buf.at[0],
                    dst_ref=buf.at[i + 1],
                    send_sem=send.at[i],
                    recv_sem=recv.at[i],
                    device_id=(t, me),
                    device_id_type=MESH,
                )
            )
            copies[-1].start()
        for copy in copies:
            copy.wait_recv()
        total = buf[0]
        for i in range(len(peers)):
            total = total + buf[i + 1]
        return total, copies

    part, copies1 = reduce(part, rbuf1, x_peers, as1, ar1)
    part, copies2 = reduce(part, rbuf2, z_peers, as2, ar2)

    aa, bb, cc, ee = (part[k : k + 1, :] for k in range(4))
    alpha = aa / bb
    rr1 = alpha * alpha * cc - aa
    beta1 = 1.0 + rr1 / aa
    alpha1 = rr1 / (beta1 * beta1 * bb - 2.0 * beta1 * alpha * cc + alpha * alpha * ee)
    coef_s = alpha + alpha1 * beta1
    coef_t = alpha1 * alpha
    both = jnp.where(row8 == 0, coef_s, coef_t)
    both = jnp.where(lax.broadcasted_iota(jnp.int32, (8, ED), 1) < SYS, both, 0.0)
    both = jnp.transpose(jnp.concatenate([both] + [jnp.zeros((8, ED), F32)] * 15, axis=0))
    coef_out[0] = jnp.broadcast_to(both[0:SYS, 0:1], (SYS, ED))
    coef_out[1] = jnp.broadcast_to(both[0:SYS, 1:2], (SYS, ED))

    def drain(a, carry):
        for i in range(NP - 1):
            copy1(a, i).wait_send()
            copy2(a, i).wait_send()
        return carry

    lax.fori_loop(0, N, drain, 0)
    for kind in (0, 1):
        for way in (0, 1):
            halo(kind, way).wait_send()
    for copy in copies1 + copies2:
        copy.wait_send()
    r_copy.wait()
    q_copy.wait()
    p_copy.wait()


def finish_kernel(r, q, p, coef, x_out, r_out):
    s, t = coef[0], coef[1]
    for n in range(N * N):
        r_n, q_n, p_n = r[n], q[n], p[n]
        x_out[pl.ds(n, 8, stride=N * N), :] = s * r_n - t * q_n
        r_out[pl.ds(n, 8, stride=N * N), :] = r_n - s * q_n + t * p_n


def on_device(velocity, elem_scale, elem_ids, edge_blocks):
    vel = velocity.reshape(SYS * N * N, ED)
    wlane = jnp.asarray(np.repeat(WEIGHTS, EG)[None, :], F32)
    fmat = jnp.asarray(halves(mode_matrix()))
    dkron = jnp.asarray(halves(np.kron(DERIV.T, np.eye(EG))))
    dtab = np.zeros((N + 1, N))
    dtab[:N] = -WEIGHTS[:, None] * DERIV
    dtab[N] = WEIGHTS
    dtab = jnp.asarray(dtab, F32)
    vmem = pl.BlockSpec(memory_space=pltpu.VMEM)
    hbm = pl.BlockSpec(memory_space=pl.ANY)
    field = jax.ShapeDtypeStruct((N * N, SYS, ED), F32)
    dma = pltpu.SemaphoreType.DMA
    r0, q0, p0, coef = pl.pallas_call(
        kernel,
        out_shape=(field, field, field, jax.ShapeDtypeStruct((2, SYS, ED), F32)),
        in_specs=[hbm, vmem, vmem, vmem, vmem, vmem, pl.BlockSpec(memory_space=pltpu.SMEM)],
        out_specs=(hbm, hbm, hbm, vmem),
        scratch_shapes=[
            pltpu.VMEM((SYS * N * N, ED), F32),
            pltpu.VMEM((N, NP, 3, ZL, ED), F32),
            pltpu.VMEM((N, 3, Z, ED), F32),
            pltpu.VMEM((N, 3, Z, ED), F32),
            pltpu.VMEM((N, 2, 3, Z, ED), BF16),
            pltpu.VMEM((N, 3, Z, ED), F32),
            pltpu.VMEM((N, NP, 3, ZL, ED), F32),
            pltpu.VMEM((N * N, SYS, ED), F32),
            pltpu.VMEM((N * N, SYS, ED), F32),
            pltpu.VMEM((N * N, SYS, ED), F32),
            pltpu.VMEM((8, ED), F32),
            pltpu.VMEM((SYS, ED), F32),
            pltpu.VMEM((12, ED, ED), BF16),
            pltpu.VMEM((4, N, SYS, ED), F32),
            pltpu.VMEM((2, N, SYS, ED), F32),
            pltpu.VMEM((2, 2, N // 2, SYS, ED), F32),
            pltpu.VMEM((2, 2, N // 2, SYS, ED), F32),
            pltpu.VMEM((4, ED, ED), F32),
            pltpu.VMEM((NX, 8, ED), F32),
            pltpu.VMEM((NZ, 8, ED), F32),
            dma,
            dma((3,)),
            dma((N, NP - 1)),
            dma((N, NP - 1)),
            dma((N, NP - 1)),
            dma((N, NP - 1)),
            dma((2, 2)),
            dma((2, 2)),
            dma((NX - 1,)),
            dma((NX - 1,)),
            dma((NZ - 1,)),
            dma((NZ - 1,)),
        ],
        compiler_params=pltpu.CompilerParams(
            collective_id=0, has_side_effects=True, vmem_limit_bytes=48 * 1024 * 1024
        ),
        name="exchange_and_apply",
    )(vel, elem_scale, elem_ids, wlane, fmat, dkron, dtab)

    block = pl.BlockSpec((N * N, 8, ED), lambda i: (0, i, 0))
    out_block = pl.BlockSpec((8 * N * N, ED), lambda i: (i, 0))
    flat = jax.ShapeDtypeStruct((SYS * N * N, ED), F32)
    new, left = pl.pallas_call(
        finish_kernel,
        grid=(SYS // 8,),
        out_shape=(flat, flat),
        in_specs=[block, block, block, pl.BlockSpec((2, 8, ED), lambda i: (0, i, 0))],
        out_specs=(out_block, out_block),
        compiler_params=pltpu.CompilerParams(vmem_limit_bytes=16 * 1024 * 1024),
        name="finish",
    )(r0, q0, p0, coef)
    shape = (3, ZL, N, N, ED)
    return new.reshape(shape), left.reshape(shape)


def solution(mesh):
    in_specs = (
        P(None, "plane", None, None, "elem"),
        P(None, "elem"),
        P("elem", None),
        P("elem", None, None),
    )
    out_specs = (P(None, "plane", None, None, "elem"), P(None, "plane", None, None, "elem"))
    return jax.shard_map(
        on_device, mesh=mesh, in_specs=in_specs, out_specs=out_specs, check_vma=False
    )
```

time: 451 us -> 78.2 us (0.17)
  blocking collectives: 217 us -> 0 us
  waiting for transfers between devices: 74.5 us -> 0 us
  Pallas kernels: 0 us -> 72.9 us
  local copies, waits for them, and re-layouts: 64.1 us -> 4.42 us
  other arithmetic: 45.4 us -> 0 us
  matrix products: 23.8 us -> 0 us
  starting transfers between devices: 22.4 us -> 0 us
    psum x3 -> x0, blocking collectives: 217 us -> none  [the longest x2 148 us: squares(): return lax.psum(inner_dot(residual, residual), 'elem')]
    all_to_all x2 -> x0, waiting for transfers between devices: 74.5 us -> none  [the longest x1 53.4 us: on_device(): lax.all_to_all(spectral, 'plane', split_axis=1, concat_axis=2, tiled=True)]
    pallas_call x0 -> x2, Pallas kernels: none -> 72.9 us  [the longest x1 68.9 us: on_device(): pl.pallas_call(kernel, out_shape=(field, field, field, jax.ShapeDtypeStru...]
    dot_general x13 -> x0, matrix products: 23.8 us -> none  [the longest x1 7.11 us: on_device(): spectral = jnp.einsum('mz,fzabe->fmabe', fourier, fields, precision=highest)]
    scatter-add x4 -> x0, local copies, waits for them, and re-layouts: 19.9 us -> none  [helmholtz(): result.at[:, 0, :, :].add(coupling[:, :, 0]).at[:, -1, :, :]]
    scatter-add x8 -> x0, other arithmetic: 18.7 us -> none  [the longest x4 13.3 us: helmholtz(): facing.at[:, blocks[0]].add(from_below).at[:, blocks[1]].add(from_above)]
    ppermute x4 -> x0, starting transfers between devices: 13 us -> none  [passed_along(): return lax.ppermute(array, axis, pairs)]
    all_to_all x2 -> x0, starting transfers between devices: 9.4 us -> none  [the longest x1 4.93 us: on_device(): lax.all_to_all(spectral, 'plane', split_axis=1, concat_axis=2, tiled=True)]
  transfers between devices with their start and end apart: 6 -> 0, of which waited for: 2 -> 0; matrix products, arithmetic and copies ran while one was open for 5% -> 0% of each run, Pallas kernels for 0% -> 0%
where the time goes in v1:
time: 78.2 us; the launch traced here: 78 us
  Pallas kernels  72.9 us (93%)
  local copies, waits for them, and re-layouts  4.42 us (6%)
    pallas_call x1, Pallas kernels, on_device(): pl.pallas_call(kernel, out_shape=(field, field, field, jax.ShapeDtypeStru...  68.9 us
    unnamed x12, local copies, waits for them, and re-layouts  4.42 us
    pallas_call x1, Pallas kernels, on_device(): pl.pallas_call(finish_kernel, grid=(SYS // 8,), out_shape=(flat, flat), i...  4.04 us

profile of v1, /device:TPU:2, one launch (start us, length us, event | category | flops | bytes accessed | tf_op | source)
XLA Modules:
  0.0 78.0 jit_solution(11594790534042451481)
XLA Ops:
  0.6 0.0 copy-start
  0.6 0.9 %copy-done = bf16[2,128,256]{2,1,0:T(8,128)(2,1)S(1)} copy-done((bf16[2,128,256]{2,1,0:T(8,128)(2,1)S(1)}, bf16[2,128,256]{2,1,0:T(8,128)(2,1)}, u32[]{:S(2)}) %copy-start) | copy-done | bytes 131096
  1.5 0.0 copy-start.1
  1.5 0.8 %copy-done.1 = bf16[2,128,128]{2,1,0:T(8,128)(2,1)S(1)} copy-done((bf16[2,128,128]{2,1,0:T(8,128)(2,1)S(1)}, bf16[2,128,128]{2,1,0:T(8,128)(2,1)}, u32[]{:S(2)}) %copy-start.1) | copy-done | bytes 65560
  2.4 0.0 copy-start.2
  2.4 0.7 copy-done.2
  3.1 0.0 copy-start.3
  3.1 0.7 copy-done.3
  3.8 0.0 copy-start.4
  3.8 0.7 copy-done.4
  4.4 0.0 copy-start.5
  4.4 0.7 copy-done.5
  5.1 68.9 %exchange_and_apply.1 = (f32[64,48,128]{2,1,0:T(8,128)S(1)}, f32[64,48,128]{2,1,0:T(8,128)S(1)}, f32[64,48,128]{2,1,0:T(8,128)S(1)}, f32[2,48,128]{2,1,0:T(8,128)S(1)}) custom-call(f32[3072,128]{1,0:T(8,128)} %bitcast.3, f32[2,128]{1,0:T(2,128)S(1)} %copy-done.3, s32[1,128]{1,0:T(1,128)S(1)} %copy-done.4, f32[1,128]{1,0:T(1,128)S(1)} %copy-done.5, ...), custom_call_target="tpu_custom_call" | custom-call | tf_op jit(solution)/shard_map/exchange_and_apply/pallas_call | solution.py:511
  73.9 4.0 %finish.1 = (f32[3072,128]{1,0:T(8,128)}, f32[3072,128]{1,0:T(8,128)}) custom-call(f32[64,48,128]{2,1,0:T(8,128)S(1)} %get-tuple-element.8.r, f32[64,48,128]{2,1,0:T(8,128)S(1)} %get-tuple-element.9.q, f32[64,48,128]{2,1,0:T(8,128)S(1)} %get-tuple-element.10.p, f32[2,48,128]{2,1,0:T(8,128)S(1)} %get-tuple-element.11.coef), custom_call_target="tpu_custom_call" | custom-call | tf_op jit(solution)/shard_map/finish/pallas_call | solution.py:559
Async XLA Ops:
  0.6 0.9 %copy-start = (bf16[2,128,256]{2,1,0:T(8,128)(2,1)S(1)}, bf16[2,128,256]{2,1,0:T(8,128)(2,1)}, u32[]{:S(2)}) copy-start(bf16[2,128,256]{2,1,0:T(8,128)(2,1)} %constant.9.clone.fmat) | copy-start | bytes 393220
  1.5 0.8 %copy-start.1 = (bf16[2,128,128]{2,1,0:T(8,128)(2,1)S(1)}, bf16[2,128,128]{2,1,0:T(8,128)(2,1)}, u32[]{:S(2)}) copy-start(bf16[2,128,128]{2,1,0:T(8,128)(2,1)} %constant.10.clone.dkron) | copy-start | bytes 196612
  2.4 0.7 copy-start.2
  3.1 0.7 copy-start.3
  3.8 0.7 copy-start.4
  4.4 0.7 copy-start.5

commit v2 on v1

v2 whole, which is shorter than its diff:
```python
import functools
import math

import jax
import jax.numpy as jnp
import ml_dtypes
import numpy as np
from jax import lax
from jax.experimental import pallas as pl
from jax.experimental.pallas import tpu as pltpu
from jax.sharding import PartitionSpec as P

MESH = pl.DeviceIdType.MESH
F32 = jnp.float32
BF16 = jnp.bfloat16

N = 8
ED = 128
Z = 128
NP = 8
ZL = Z // NP
EG = ED // NP
SYS = 3 * ZL
NX = 4
NZ = 8
NE = NX * NZ
PAIRS = N // 2
PEN = 8.0
ROW_W = N * N
ROW_LANE = ROW_W + N
ROWS = 80
LAM = 4.0
STEP = 0.1


def node_tables():
    degree = N - 1
    points = -np.cos(np.pi * np.arange(N) / degree)
    scales = np.ones(N)
    scales[0] = 2.0
    scales[-1] = 2.0
    bary = (-1.0) ** np.arange(N) / scales
    deriv = np.zeros((N, N))
    for i in range(N):
        for j in range(N):
            if i != j:
                deriv[i, j] = bary[j] / bary[i] / (points[i] - points[j])
        deriv[i, i] = -np.sum(deriv[i])
    weights = np.zeros(N)
    for i in range(N):
        running = 0.0
        for k in range(1, degree // 2 + 1):
            factor = 1.0 if 2 * k == degree else 2.0
            running += factor / (4.0 * k * k - 1.0) * np.cos(2.0 * np.pi * i * k / degree)
        weights[i] = (1.0 if i in (0, degree) else 2.0) / degree * (1.0 - running)
    stiff = deriv.T @ (weights[:, None] * deriv)
    return deriv, weights, stiff


def mode_matrix():
    slots = np.arange(Z)
    harmonic = slots // 2
    angles = 2.0 * math.pi / Z * (harmonic[:, None] * slots[None, :] % Z)
    four = np.where((slots % 2 == 0)[:, None], np.cos(angles), np.sin(angles)) * (2.0 / Z)
    four[0] = 1.0 / Z
    four[1] = np.where(slots % 2 == 0, 1.0, -1.0) / Z
    dz = np.zeros((Z, Z))
    wave = STEP * np.arange(Z // 2)
    dz[0::2] = wave[:, None] * four[1::2]
    dz[1::2] = -wave[:, None] * four[0::2]
    return np.concatenate([four, -dz], axis=1)


def halves(table):
    high = table.astype(np.float32).astype(ml_dtypes.bfloat16)
    low = (table - high.astype(np.float64)).astype(np.float32).astype(ml_dtypes.bfloat16)
    return np.stack([high, low])


DERIV, WEIGHTS, STIFF = node_tables()


def split(x):
    high = x.astype(BF16)
    return high, (x - high.astype(F32)).astype(BF16)


def dot(x, y):
    return jnp.dot(x, y, preferred_element_type=F32)


def pick(x, table):
    high, low = split(x)
    return dot(high, table) + dot(low, table)


def block_transpose(rows):
    rows = list(rows)
    lane = lax.broadcasted_iota(jnp.int32, rows[0].shape, rows[0].ndim - 1) // EG
    for d in (1, 2, 4):
        clear = (lane & d) == 0
        for i in range(NP):
            if i & d == 0:
                x, y = rows[i], rows[i + d]
                axis = x.ndim - 1
                rows[i] = jnp.where(clear, x, pltpu.roll(y, EG * d, axis))
                rows[i + d] = jnp.where(clear, pltpu.roll(x, ED - EG * d, axis), y)
    return rows


def stiff_times(v):
    even = [v[p] + v[N - 1 - p] for p in range(N // 2)]
    odd = [v[p] - v[N - 1 - p] for p in range(N // 2)]
    out = [None] * N
    for a in range(N // 2):
        s = [0.5 * (STIFF[a, p] + STIFF[a, N - 1 - p]) for p in range(N // 2)]
        t = [0.5 * (STIFF[a, p] - STIFF[a, N - 1 - p]) for p in range(N // 2)]
        e = sum(float(s[p]) * even[p] for p in range(1, N // 2)) + float(s[0]) * even[0]
        o = sum(float(t[p]) * odd[p] for p in range(1, N // 2)) + float(t[0]) * odd[0]
        out[a] = e + o
        out[N - 1 - a] = e - o
    return out


def kernel(
    vel,
    scale_in,
    ids_in,
    rows_in,
    mats_in,
    res,
    qv,
    pv,
    coef_out,
    vin,
    scale,
    ids,
    ctab,
    mats,
    xsend,
    xbuf,
    acc,
    bbuf,
    fsend,
    fbuf,
    geo,
    hel,
    tables,
    face,
    edge,
    hsend,
    hrecv,
    dots,
    rbuf,
    in_sem,
    s1,
    r1,
    s2,
    r2,
    hs,
    hr,
    rs,
    rr,
):
    e = lax.axis_index("elem")
    me = lax.axis_index("plane")
    y, core = me // 2, lax.rem(me, 2)
    z, x = e // NX, lax.rem(e, NX)
    plane_offsets = [(dy, dc) for dy in (2, 1, 3, 0) for dc in (0, 1) if (dy, dc) != (0, 0)]
    plane_peers = [lax.rem(y + dy, 4) * 2 + lax.rem(core + dc, 2) for dy, dc in plane_offsets]
    elem_peers = [
        lax.rem(z + dz, NZ) * NX + lax.rem(x + dx, NX)
        for dz in (4, 3, 5, 2, 6, 1, 7, 0)
        for dx in (2, 1, 3, 0)
        if (dz, dx) != (0, 0)
    ]
    up, down = lax.rem(e + 1, NE), lax.rem(e + NE - 1, NE)

    pairs = ((vel, vin), (scale_in, scale), (ids_in, ids), (rows_in, ctab), (mats_in, mats))
    loads = [pltpu.make_async_copy(src, dst, in_sem.at[i]) for i, (src, dst) in enumerate(pairs)]
    for load in loads:
        load.start()
    barrier = pltpu.get_barrier_semaphore()
    for t in plane_peers:
        pl.semaphore_signal(barrier, inc=1, device_id=(e, t), device_id_type=MESH)
    for t in elem_peers:
        pl.semaphore_signal(barrier, inc=1, device_id=(t, me), device_id_type=MESH)

    for load in loads[1:]:
        load.wait()

    lid = ids[...] & (ED - 1)
    growth = 1.0 + 2.0 * (ids[...] // 64).astype(F32) / 63.0
    circ = scale[0:1, :] * growth
    radial = scale[1:2, :]
    geo[0:1, :] = circ * radial
    geo[1:2, :] = radial / circ
    geo[2:3, :] = circ / radial
    lane_row = lax.broadcasted_iota(jnp.int32, (1, ED), 1)
    for k, val in ((3, circ), (4, radial)):
        val = pltpu.roll(jnp.broadcast_to(val, (8, ED)), lax.rem(ED - EG * me, ED), 1)
        val = jnp.where(lax.broadcasted_iota(jnp.int32, (8, ED), 1) < EG, val, 0.0)
        for d in (1, 2, 4):
            val = val + pltpu.roll(val, EG * d, 1)
        geo[k : k + 1, :] = val[0:1, :]
    wl = ctab[ROW_LANE : ROW_LANE + 1, :]
    g_circ, g_radial = geo[3:4, :], geo[4:5, :]
    geo[5:6, :] = g_circ * g_radial * wl
    geo[6:7, :] = g_circ * wl
    geo[7:8, :] = g_radial * wl
    loads[0].wait()
    pl.semaphore_wait(barrier, NP - 1 + NE - 1)

    def copy1(a, i):
        t = plane_peers[i]
        return pltpu.make_async_remote_copy(
            src_ref=xsend.at[a, t],
            dst_ref=xbuf.at[a, :, pl.ds(pl.multiple_of(me * ZL, ZL), ZL), :],
            send_sem=s1.at[a, i],
            recv_sem=r1.at[a, i],
            device_id=(e, t),
            device_id_type=MESH,
        )

    def copy2(c, pair, i):
        t = plane_peers[i]
        return pltpu.make_async_remote_copy(
            src_ref=fsend.at[c, pl.ds(2 * pair, 2), pl.ds(pl.multiple_of(t * ZL, ZL), ZL), :],
            dst_ref=fbuf.at[c, me, pl.ds(2 * pair, 2)],
            send_sem=s2.at[c, pair, i],
            recv_sem=r2.at[c, pair, i],
            device_id=(e, t),
            device_id_type=MESH,
        )

    def send_first(a, carry):
        for c in range(3):
            for h in range(ZL // 8):
                base = (c * ZL + h * 8) * N * N + a * N
                rows = [vin[pl.ds(base + b, 8, stride=N * N), :] for b in range(N)]
                for q, row in enumerate(block_transpose(rows)):
                    xsend[a, q, c, pl.ds(h * 8, 8), :] = row
        for i in range(NP - 1):
            copy1(a, i).start()
        mine = pl.ds(pl.multiple_of(me * ZL, ZL), ZL)
        xbuf[a, :, mine, :] = xsend[a, me]
        return carry

    lax.fori_loop(0, N, send_first, 0)

    acc[...] = jnp.zeros_like(acc)
    dots[...] = jnp.zeros_like(dots)
    row_i = lax.broadcasted_iota(jnp.int32, (ED, ED), 0)
    lane_i = lax.broadcasted_iota(jnp.int32, (ED, ED), 1)
    lid_l = jnp.broadcast_to(lid, (ED, ED))
    lid_t = jnp.transpose(lid_l.astype(F32)).astype(jnp.int32)

    def ones(where):
        return jnp.where(where, 1.0, 0.0).astype(BF16)

    tables[0] = ones(lid_t == ((lid_l & 64) | ((lid_l + 63) & 63)))
    tables[1] = ones(lid_t == ((lid_l & 64) | ((lid_l + 1) & 63)))
    tables[2] = ones((lid_t == (lid_l ^ 64)) & (lid_l >= 64))
    tables[3] = ones((lid_t == (lid_l ^ 64)) & (lid_l < 64))
    tables[4] = ones(lid_t == lane_i + 64)
    tables[5] = ones((lid_t == lane_i) & (lane_i >= 64))
    tables[6] = ones((lid_t == lane_i) & (lane_i < 64))
    tables[7] = ones(lid_t + 64 == lane_i)
    tables[8] = ones((row_i == lid_l) & (lid_l < 64))
    tables[9] = ones(row_i == lid_l + 64)
    tables[10] = ones(row_i + 64 == lid_l)
    tables[11] = ones((row_i == lid_l) & (lid_l >= 64))
    slot = me * ZL + (lax.broadcasted_iota(jnp.int32, (SYS, ED), 0) & (ZL - 1))
    kappa = jnp.where(slot == 1, Z // 2, slot // 2).astype(F32)
    hel[...] = (LAM + (STEP * kappa) * (STEP * kappa)) * geo[0:1, :]

    def arrive_first(p, carry):
        for i in range(NP - 1):
            copy1(p, i).wait_recv()
        w_p = ctab[pl.ds(ROW_W + p, 1), :]
        mass = geo[5:6, :] * w_p
        g_y = geo[6:7, :] * w_p
        g_x = geo[7:8, :]
        for c in range(3):
            fy_high, fy_low = split(xbuf[p, 1] * xbuf[p, c])
            dy = dot(fy_high, mats[4]) + dot(fy_low, mats[4]) + dot(fy_high, mats[5])
            acc[p, c] += (LAM * mass) * xbuf[p, c] - g_y * dy
            b_high, b_low = split(mass * (xbuf[p, 2] * xbuf[p, c]))
            bbuf[p, 0, c] = b_high
            bbuf[p, 1, c] = b_low
            for h in range(4):
                rows = pl.ds(h * 32, 32)
                fx = g_x * (xbuf[p, 0, rows, :] * xbuf[p, c, rows, :])
                for a in range(N):
                    acc[a, c, rows, :] += ctab[pl.ds(p * N + a, 1), :] * fx
        return carry

    lax.fori_loop(0, N, arrive_first, 0)

    f_high = jnp.concatenate([mats[0], mats[1]], axis=1)
    f_low = jnp.concatenate([mats[2], mats[3]], axis=1)

    def send_second(step, carry):
        c, pair = step // PAIRS, lax.rem(step, PAIRS)
        for k in (0, 1):
            a = 2 * pair + k
            a_high, a_low = split(acc[a, c])
            high = jnp.concatenate([a_high, bbuf[a, 0, c]], axis=0)
            low = jnp.concatenate([a_low, bbuf[a, 1, c]], axis=0)
            fsend[c, a] = dot(f_high, high) + dot(f_high, low) + dot(f_low, high)
        for i in range(NP - 1):
            copy2(c, pair, i).start()
        mine = pl.ds(pl.multiple_of(me * ZL, ZL), ZL)
        fbuf[c, me, pl.ds(2 * pair, 2)] = fsend[c, pl.ds(2 * pair, 2), mine, :]
        return carry

    lax.fori_loop(0, 3 * PAIRS, send_second, 0)

    def sys_rows(c):
        return pl.ds(pl.multiple_of(c * ZL, ZL), ZL)

    def halo(c, kind, way):
        return pltpu.make_async_remote_copy(
            src_ref=hsend.at[c, kind, way],
            dst_ref=hrecv.at[c, kind, way],
            send_sem=hs.at[c, kind, way],
            recv_sem=hr.at[c, kind, way],
            device_id=((up, down)[way], me),
            device_id_type=MESH,
        )

    def side(v, rows, b, first, count):
        return jnp.concatenate([v[a * N + b, rows, :] for a in range(first, first + count)], axis=0)

    def send_edges(v, c, kind):
        rows = sys_rows(c)
        for way, b, t in ((0, N - 1, 4), (1, 0, 6)):
            got = pick(side(v, rows, b, 0, N // 2), tables[t])
            got = got + pick(side(v, rows, b, N // 2, N // 2), tables[t + 1])
            hsend[c, kind, way] = got.reshape(N // 2, ZL, ED)
            halo(c, kind, way).start()

    def take_edges(c, kind):
        for way in (0, 1):
            halo(c, kind, way).wait_recv()
            there = (e > 0) if way == 0 else (e < NE - 1)
            for half in (0, 1):
                got = hrecv[c, kind, way].reshape(N // 2 * ZL, ED)
                got = pick(got, tables[8 + 2 * way + half])
                got = jnp.where(there, got, 0.0)
                edge[way, pl.ds(half * (N // 2), N // 2)] = got.reshape(N // 2, ZL, ED)

    def apply_local(v, q, c):
        sys = sys_rows(c)
        shape = (N, ZL, ED)
        face[0] = pick(v[(N - 1) * N : N * N, sys, :].reshape(N * ZL, ED), tables[0]).reshape(shape)
        face[1] = pick(v[0:N, sys, :].reshape(N * ZL, ED), tables[1]).reshape(shape)
        face[2] = pick(side(v, sys, N - 1, 0, N), tables[2]).reshape(shape)
        face[3] = pick(side(v, sys, 0, 0, N), tables[3]).reshape(shape)

        def tile(h, carry):
            rows = pl.ds(pl.multiple_of(c * ZL + h * 8, 8), 8)
            frows = pl.ds(pl.multiple_of(h * 8, 8), 8)
            hm = hel[rows, :]
            kx = jnp.broadcast_to(geo[1:2, :], (8, ED))
            ky = jnp.broadcast_to(geo[2:3, :], (8, ED))
            for b in range(N):
                col = stiff_times([v[a * N + b, rows, :] for a in range(N)])
                scale_b = kx * float(WEIGHTS[b])
                for a in range(N):
                    q[a * N + b, rows, :] = scale_b * col[a]
            for a in range(N):
                vals = [v[a * N + b, rows, :] for b in range(N)]
                line = stiff_times(vals)
                scale_a = ky * float(WEIGHTS[a])
                hm_a = hm * float(WEIGHTS[a])
                for b in range(N):
                    out = q[a * N + b, rows, :] + scale_a * line[b]
                    out = out + (hm_a * float(WEIGHTS[b])) * vals[b]
                    if a == 0:
                        out = out + float(PEN * WEIGHTS[b]) * (vals[b] - face[0, b, frows, :])
                    if a == N - 1:
                        out = out + float(PEN * WEIGHTS[b]) * (vals[b] - face[1, b, frows, :])
                    if b == 0:
                        out = out + float(PEN * WEIGHTS[a]) * (vals[b] - face[2, a, frows, :])
                    if b == N - 1:
                        out = out + float(PEN * WEIGHTS[a]) * (vals[b] - face[3, a, frows, :])
                    q[a * N + b, rows, :] = out
            return carry

        lax.fori_loop(0, ZL // 8, tile, 0)

    def add_edges(q, c):
        rows = sys_rows(c)
        for a in range(N):
            q[a * N, rows, :] -= float(PEN * WEIGHTS[a]) * edge[0, a]
            q[a * N + N - 1, rows, :] -= float(PEN * WEIGHTS[a]) * edge[1, a]

    def arrive_second(c):
        def row(a, carry):
            for h in range(ZL // 8):
                rows = [fbuf[c, s, a, pl.ds(h * 8, 8), :] for s in range(NP)]
                for b, line in enumerate(block_transpose(rows)):
                    res[a * N + b, pl.ds(pl.multiple_of(c * ZL + h * 8, 8), 8), :] = line
            return carry

        def pair(k, carry):
            for i in range(NP - 1):
                copy2(c, k, i).wait_recv()
            return lax.fori_loop(2 * k, 2 * k + 2, row, carry)

        lax.fori_loop(0, PAIRS, pair, 0)

    def begin(c):
        arrive_second(c)
        send_edges(res, c, 0)
        apply_local(res, qv, c)
        send_edges(qv, c, 1)

    def end(c):
        take_edges(c, 0)
        add_edges(qv, c)
        apply_local(qv, pv, c)
        take_edges(c, 1)
        rows = sys_rows(c)
        inner = jnp.broadcast_to(lid < 64, (ZL, ED)) & (e > 0)
        outer = jnp.broadcast_to(lid >= 64, (ZL, ED)) & (e < NE - 1)
        for a in range(N):
            w_a = float(PEN * WEIGHTS[a])
            edge[0, a] -= jnp.where(inner, w_a * res[a * N, rows, :], 0.0)
            edge[1, a] -= jnp.where(outer, w_a * res[a * N + N - 1, rows, :], 0.0)
        add_edges(pv, c)

        def dot_tile(h, carry):
            rows = pl.ds(pl.multiple_of(c * ZL + h * 8, 8), 8)
            sums = [jnp.zeros((8, ED), F32) for _ in range(4)]
            for n in range(N * N):
                r_n, q_n, p_n = res[n, rows, :], qv[n, rows, :], pv[n, rows, :]
                for k, prod in enumerate((r_n * r_n, r_n * q_n, q_n * q_n, q_n * p_n)):
                    sums[k] = sums[k] + prod
            for k in range(4):
                dots[k, rows, :] = sums[k]
            return carry

        lax.fori_loop(0, ZL // 8, dot_tile, 0)

    begin(0)

    def component(c, carry):
        begin(c)
        end(c - 1)
        return carry

    lax.fori_loop(1, 3, component, 0)
    end(2)

    one_rows = jnp.ones((8, ED), F32)
    row8 = lax.broadcasted_iota(jnp.int32, (8, ED), 0)
    part = jnp.zeros((8, ED), F32)
    for k in range(4):
        summed = lax.dot_general(
            one_rows,
            dots[k],
            (((1,), (1,)), ((), ())),
            precision=lax.Precision.HIGHEST,
            preferred_element_type=F32,
        )
        part = jnp.where(row8 == k, summed, part)

    rbuf[0] = part

    def spread(i):
        return pltpu.make_async_remote_copy(
            src_ref=rbuf.at[0],
            dst_ref=rbuf.at[i + 1],
            send_sem=rs.at[i],
            recv_sem=rr.at[i],
            device_id=(elem_peers[i], me),
            device_id_type=MESH,
        )

    for i in range(NE - 1):
        spread(i).start()
    for i in range(NE - 1):
        spread(i).wait_recv()
    part = jnp.sum(rbuf[...], axis=0)

    aa, bb, cc, ee = (part[k : k + 1, :] for k in range(4))
    alpha = aa / bb
    rr1 = alpha * alpha * cc - aa
    beta1 = 1.0 + rr1 / aa
    alpha1 = rr1 / (beta1 * beta1 * bb - 2.0 * beta1 * alpha * cc + alpha * alpha * ee)
    coef_s = alpha + alpha1 * beta1
    coef_t = alpha1 * alpha
    both = jnp.where(row8 == 0, coef_s, coef_t)
    both = jnp.where(lax.broadcasted_iota(jnp.int32, (8, ED), 1) < SYS, both, 0.0)
    both = jnp.transpose(jnp.concatenate([both] + [jnp.zeros((8, ED), F32)] * 15, axis=0))
    coef_out[0] = jnp.broadcast_to(both[0:SYS, 0:1], (SYS, ED))
    coef_out[1] = jnp.broadcast_to(both[0:SYS, 1:2], (SYS, ED))

    def drain(a, carry):
        for i in range(NP - 1):
            copy1(a, i).wait_send()
        return carry

    def drain2(step, carry):
        for i in range(NP - 1):
            copy2(step // PAIRS, lax.rem(step, PAIRS), i).wait_send()
        return carry

    def drain3(c, carry):
        for kind in (0, 1):
            for way in (0, 1):
                halo(c, kind, way).wait_send()
        return carry

    lax.fori_loop(0, N, drain, 0)
    lax.fori_loop(0, 3 * PAIRS, drain2, 0)
    lax.fori_loop(0, 3, drain3, 0)
    for i in range(NE - 1):
        spread(i).wait_send()


def finish_kernel(r, q, p, coef, x_out, r_out, xs, rs, sem):
    def tile(st, carry):
        rows = pl.ds(pl.multiple_of(st * 8, 8), 8)
        s, t = coef[0, rows, :], coef[1, rows, :]
        for n in range(N * N):
            r_n, q_n, p_n = r[n, rows, :], q[n, rows, :], p[n, rows, :]
            xs[st, pl.ds(n, 8, stride=N * N), :] = s * r_n - t * q_n
            rs[st, pl.ds(n, 8, stride=N * N), :] = r_n - s * q_n + t * p_n
        for copy in out_copies(st):
            copy.start()
        return carry

    def out_copies(st):
        return (
            pltpu.make_async_copy(xs.at[st], x_out.at[st], sem.at[st, 0]),
            pltpu.make_async_copy(rs.at[st], r_out.at[st], sem.at[st, 1]),
        )

    def drain(st, carry):
        for copy in out_copies(st):
            copy.wait()
        return carry

    lax.fori_loop(0, SYS // 8, tile, 0)
    lax.fori_loop(0, SYS // 8, drain, 0)


def on_device(velocity, elem_scale, elem_ids, edge_blocks):
    vel = velocity.reshape(SYS * N * N, ED)
    rows = np.zeros((ROWS, ED))
    rows[: N * N] = (-WEIGHTS[:, None] * DERIV).T.reshape(N * N, 1)
    rows[ROW_W : ROW_W + N] = WEIGHTS[:, None]
    rows[ROW_LANE] = np.repeat(WEIGHTS, EG)
    rows = jnp.asarray(rows, F32)
    four = halves(mode_matrix()).reshape(2, Z, 2, Z).transpose(0, 2, 1, 3).reshape(4, Z, Z)
    mats = jnp.asarray(np.concatenate([four, halves(np.kron(DERIV.T, np.eye(EG)))]))
    operands = (vel, elem_scale, elem_ids, rows, mats)
    vmem = pl.BlockSpec(memory_space=pltpu.VMEM)
    hbm = pl.BlockSpec(memory_space=pltpu.HBM)
    field = jax.ShapeDtypeStruct((N * N, SYS, ED), F32)
    dma = pltpu.SemaphoreType.DMA
    r0, q0, p0, coef = pl.pallas_call(
        kernel,
        out_shape=(field, field, field, jax.ShapeDtypeStruct((2, SYS, ED), F32)),
        in_specs=[hbm] * 5,
        out_specs=(vmem,) * 4,
        scratch_shapes=[
            pltpu.VMEM((SYS * N * N, ED), F32),
            pltpu.VMEM((2, ED), F32),
            pltpu.VMEM((1, ED), jnp.int32),
            pltpu.VMEM((ROWS, ED), F32),
            pltpu.VMEM((6, ED, ED), BF16),
            pltpu.VMEM((N, NP, 3, ZL, ED), F32),
            pltpu.VMEM((N, 3, Z, ED), F32),
            pltpu.VMEM((N, 3, Z, ED), F32),
            pltpu.VMEM((N, 2, 3, Z, ED), BF16),
            pltpu.VMEM((3, N, Z, ED), F32),
            pltpu.VMEM((3, NP, N, ZL, ED), F32),
            pltpu.VMEM((8, ED), F32),
            pltpu.VMEM((SYS, ED), F32),
            pltpu.VMEM((12, ED, ED), BF16),
            pltpu.VMEM((4, N, ZL, ED), F32),
            pltpu.VMEM((2, N, ZL, ED), F32),
            pltpu.VMEM((3, 2, 2, N // 2, ZL, ED), F32),
            pltpu.VMEM((3, 2, 2, N // 2, ZL, ED), F32),
            pltpu.VMEM((4, ED, ED), F32),
            pltpu.VMEM((NE, 8, ED), F32),
            dma((5,)),
            dma((N, NP - 1)),
            dma((N, NP - 1)),
            dma((3, PAIRS, NP - 1)),
            dma((3, PAIRS, NP - 1)),
            dma((3, 2, 2)),
            dma((3, 2, 2)),
            dma((NE - 1,)),
            dma((NE - 1,)),
        ],
        compiler_params=pltpu.CompilerParams(
            collective_id=0, has_side_effects=True, vmem_limit_bytes=48 * 1024 * 1024
        ),
        name="exchange_and_apply",
    )(*[pltpu.with_memory_space_constraint(v, pltpu.HBM) for v in operands])

    flat = jax.ShapeDtypeStruct((SYS // 8, 8 * N * N, ED), F32)
    new, left = pl.pallas_call(
        finish_kernel,
        out_shape=(flat, flat),
        in_specs=[vmem] * 4,
        out_specs=(hbm, hbm),
        scratch_shapes=[
            pltpu.VMEM(flat.shape, F32),
            pltpu.VMEM(flat.shape, F32),
            dma((SYS // 8, 2)),
        ],
        compiler_params=pltpu.CompilerParams(vmem_limit_bytes=16 * 1024 * 1024),
        name="finish",
    )(r0, q0, p0, coef)
    shape = (3, ZL, N, N, ED)
    return new.reshape(shape), left.reshape(shape)


def solution(mesh):
    in_specs = (
        P(None, "plane", None, None, "elem"),
        P(None, "elem"),
        P("elem", None),
        P("elem", None, None),
    )
    out_specs = (P(None, "plane", None, None, "elem"), P(None, "plane", None, None, "elem"))
    return jax.shard_map(
        on_device, mesh=mesh, in_specs=in_specs, out_specs=out_specs, check_vma=False
    )
```

time: 78.2 us -> 69.7 us (0.89)
  Pallas kernels: 72.9 us -> 68.2 us
  local copies, waits for them, and re-layouts: 4.42 us -> 0 us
    unnamed x12 -> x0, local copies, waits for them, and re-layouts: 4.42 us -> none
    pallas_call x1, Pallas kernels: 68.9 us -> 65.3 us  [on_device(): pl.pallas_call(kernel, out_shape=(field, field, field, jax.ShapeDtypeStru...]
    pallas_call x1, Pallas kernels: 4.04 us -> 2.88 us  [on_device(): pl.pallas_call(finish_kernel, out_shape=(flat, flat), in_specs=[vmem] * 4...]
where the time goes in v2:
time: 69.7 us; the launch traced here: 68.9 us
  Pallas kernels  68.2 us (98%)
    pallas_call x1, Pallas kernels, on_device(): pl.pallas_call(kernel, out_shape=(field, field, field, jax.ShapeDtypeStru...  65.3 us
    pallas_call x1, Pallas kernels, on_device(): pl.pallas_call(finish_kernel, out_shape=(flat, flat), in_specs=[vmem] * 4...  2.88 us

profile of v2, /device:TPU:2, one launch (start us, length us, event | category | flops | bytes accessed | tf_op | source)
XLA Modules:
  0.0 68.9 jit_solution(2821029593482665688)
XLA Ops:
  0.6 65.3 %exchange_and_apply.1 = (f32[64,48,128]{2,1,0:T(8,128)S(1)}, f32[64,48,128]{2,1,0:T(8,128)S(1)}, f32[64,48,128]{2,1,0:T(8,128)S(1)}, f32[2,48,128]{2,1,0:T(8,128)S(1)}) custom-call(f32[3072,128]{1,0:T(8,128)} %bitcast.3, f32[2,128]{1,0:T(2,128)} %scale_in.1, s32[1,128]{1,0:T(1,128)} %ids_in.1, f32[80,128]{1,0:T(8,128)} %constant.4.clone.rows_in, ...), custom_call_target="tpu_custom_call" | custom-call | tf_op jit(solution)/shard_map/exchange_and_apply/pallas_call | solution.py:565
  66.0 2.9 %finish.1 = (f32[6,512,128]{2,1,0:T(8,128)}, f32[6,512,128]{2,1,0:T(8,128)}) custom-call(f32[64,48,128]{2,1,0:T(8,128)S(1)} %get-tuple-element.8.r, f32[64,48,128]{2,1,0:T(8,128)S(1)} %get-tuple-element.9.q, f32[64,48,128]{2,1,0:T(8,128)S(1)} %get-tuple-element.10.p, f32[2,48,128]{2,1,0:T(8,128)S(1)} %get-tuple-element.11.coef), custom_call_target="tpu_custom_call" | custom-call | tf_op jit(solution)/shard_map/finish/pallas_call | solution.py:608

commit v3 on v2

--- a/solution.py
+++ b/solution.py
@@ -108,11 +108,11 @@
     return rows
 
 
-def stiff_times(v):
+def stiff_times(v, wanted):
     even = [v[p] + v[N - 1 - p] for p in range(N // 2)]
     odd = [v[p] - v[N - 1 - p] for p in range(N // 2)]
     out = [None] * N
-    for a in range(N // 2):
+    for a in wanted:
         s = [0.5 * (STIFF[a, p] + STIFF[a, N - 1 - p]) for p in range(N // 2)]
         t = [0.5 * (STIFF[a, p] - STIFF[a, N - 1 - p]) for p in range(N // 2)]
         e = sum(float(s[p]) * even[p] for p in range(1, N // 2)) + float(s[0]) * even[0]
@@ -148,8 +148,10 @@
     tables,
     face,
     edge,
-    hsend,
-    hrecv,
+    rsend,
+    rrecv,
+    qsend,
+    qrecv,
     dots,
     rbuf,
     in_sem,
@@ -157,8 +159,10 @@
     r1,
     s2,
     r2,
-    hs,
-    hr,
+    hs1,
+    hr1,
+    hs2,
+    hr2,
     rs,
     rr,
 ):
@@ -208,8 +212,6 @@
     geo[5:6, :] = g_circ * g_radial * wl
     geo[6:7, :] = g_circ * wl
     geo[7:8, :] = g_radial * wl
-    loads[0].wait()
-    pl.semaphore_wait(barrier, NP - 1 + NE - 1)
 
     def copy1(a, i):
         t = plane_peers[i]
@@ -233,20 +235,31 @@
             device_id_type=MESH,
         )
 
-    def send_first(a, carry):
+    def pack_first(a):
         for c in range(3):
             for h in range(ZL // 8):
-                base = (c * ZL + h * 8) * N * N + a * N
-                rows = [vin[pl.ds(base + b, 8, stride=N * N), :] for b in range(N)]
-                for q, row in enumerate(block_transpose(rows)):
+                tile = vin[pl.ds(c * ZL + h * 8, 8), pl.ds(pl.multiple_of(a * N, N), N), :]
+                tile = jnp.swapaxes(tile, 0, 1)
+                for q, row in enumerate(block_transpose([tile[b] for b in range(N)])):
                     xsend[a, q, c, pl.ds(h * 8, 8), :] = row
+
+    def send_first(a):
         for i in range(NP - 1):
             copy1(a, i).start()
         mine = pl.ds(pl.multiple_of(me * ZL, ZL), ZL)
         xbuf[a, :, mine, :] = xsend[a, me]
-        return carry
-
-    lax.fori_loop(0, N, send_first, 0)
+
+    loads[0].wait()
+    pack_first(0)
+    pl.semaphore_wait(barrier, NP - 1 + NE - 1)
+    send_first(0)
+
+    def first(a, carry):
+        pack_first(a)
+        send_first(a)
+        return carry
+
+    lax.fori_loop(1, N, first, 0)
 
     acc[...] = jnp.zeros_like(acc)
     dots[...] = jnp.zeros_like(dots)
@@ -319,62 +332,86 @@
     def sys_rows(c):
         return pl.ds(pl.multiple_of(c * ZL, ZL), ZL)
 
-    def halo(c, kind, way):
+    def r_halo(c, way, pair):
         return pltpu.make_async_remote_copy(
-            src_ref=hsend.at[c, kind, way],
-            dst_ref=hrecv.at[c, kind, way],
-            send_sem=hs.at[c, kind, way],
-            recv_sem=hr.at[c, kind, way],
+            src_ref=rsend.at[c, way, pair],
+            dst_ref=rrecv.at[c, way, pair],
+            send_sem=hs1.at[c, way, pair],
+            recv_sem=hr1.at[c, way, pair],
             device_id=((up, down)[way], me),
             device_id_type=MESH,
         )
 
+    def q_halo(c, way):
+        return pltpu.make_async_remote_copy(
+            src_ref=qsend.at[c, way],
+            dst_ref=qrecv.at[c, way],
+            send_sem=hs2.at[c, way],
+            recv_sem=hr2.at[c, way],
+            device_id=((up, down)[way], me),
+            device_id_type=MESH,
+        )
+
     def side(v, rows, b, first, count):
         return jnp.concatenate([v[a * N + b, rows, :] for a in range(first, first + count)], axis=0)
 
-    def send_edges(v, c, kind):
+    def pack_edges(v, c, pair, count):
         rows = sys_rows(c)
-        for way, b, t in ((0, N - 1, 4), (1, 0, 6)):
-            got = pick(side(v, rows, b, 0, N // 2), tables[t])
-            got = got + pick(side(v, rows, b, N // 2, N // 2), tables[t + 1])
-            hsend[c, kind, way] = got.reshape(N // 2, ZL, ED)
-            halo(c, kind, way).start()
-
-    def take_edges(c, kind):
+        packed = []
+        for b, t in ((N - 1, 4), (0, 6)):
+            for k in (0, 1):
+                nodes = [v[(2 * (pair + i) + k) * N + b, rows, :] for i in range(count)]
+                nodes = jnp.concatenate(nodes, axis=0) if count > 1 else nodes[0]
+                packed.append(pick(nodes, tables[t + k]))
+        return packed[0] + packed[1], packed[2] + packed[3]
+
+    def send_r_edges(c, pair):
+        for way, got in enumerate(pack_edges(res, c, pair, 1)):
+            rsend[c, way, pair] = got
+            r_halo(c, way, pair).start()
+
+    def send_q_edges(c):
+        for way, got in enumerate(pack_edges(qv, c, 0, PAIRS)):
+            qsend[c, way] = got.reshape(PAIRS, ZL, ED)
+            q_halo(c, way).start()
+
+    def take_edges(recv, c):
         for way in (0, 1):
-            halo(c, kind, way).wait_recv()
             there = (e > 0) if way == 0 else (e < NE - 1)
-            for half in (0, 1):
-                got = hrecv[c, kind, way].reshape(N // 2 * ZL, ED)
-                got = pick(got, tables[8 + 2 * way + half])
-                got = jnp.where(there, got, 0.0)
-                edge[way, pl.ds(half * (N // 2), N // 2)] = got.reshape(N // 2, ZL, ED)
-
-    def apply_local(v, q, c):
+            got = recv[c, way].reshape(PAIRS * ZL, ED)
+            for k in (0, 1):
+                here = jnp.where(there, pick(got, tables[8 + 2 * way + k]), 0.0)
+                here = here.reshape(PAIRS, ZL, ED)
+                for pair in range(PAIRS):
+                    edge[way, 2 * pair + k] = here[pair]
+
+    def take_faces(v, c):
         sys = sys_rows(c)
         shape = (N, ZL, ED)
+        face[2] = pick(side(v, sys, N - 1, 0, N), tables[2]).reshape(shape)
+        face[3] = pick(side(v, sys, 0, 0, N), tables[3]).reshape(shape)
         face[0] = pick(v[(N - 1) * N : N * N, sys, :].reshape(N * ZL, ED), tables[0]).reshape(shape)
         face[1] = pick(v[0:N, sys, :].reshape(N * ZL, ED), tables[1]).reshape(shape)
-        face[2] = pick(side(v, sys, N - 1, 0, N), tables[2]).reshape(shape)
-        face[3] = pick(side(v, sys, 0, 0, N), tables[3]).reshape(shape)
-
+
+    def apply_local(v, q, c, columns):
         def tile(h, carry):
             rows = pl.ds(pl.multiple_of(c * ZL + h * 8, 8), 8)
             frows = pl.ds(pl.multiple_of(h * 8, 8), 8)
             hm = hel[rows, :]
             kx = jnp.broadcast_to(geo[1:2, :], (8, ED))
             ky = jnp.broadcast_to(geo[2:3, :], (8, ED))
-            for b in range(N):
-                col = stiff_times([v[a * N + b, rows, :] for a in range(N)])
+            nodes = [b for pair in columns for b in (pair, N - 1 - pair)]
+            for b in nodes:
+                col = stiff_times([v[a * N + b, rows, :] for a in range(N)], range(N // 2))
                 scale_b = kx * float(WEIGHTS[b])
                 for a in range(N):
                     q[a * N + b, rows, :] = scale_b * col[a]
             for a in range(N):
                 vals = [v[a * N + b, rows, :] for b in range(N)]
-                line = stiff_times(vals)
+                line = stiff_times(vals, columns)
                 scale_a = ky * float(WEIGHTS[a])
                 hm_a = hm * float(WEIGHTS[a])
-                for b in range(N):
+                for b in nodes:
                     out = q[a * N + b, rows, :] + scale_a * line[b]
                     out = out + (hm_a * float(WEIGHTS[b])) * vals[b]
                     if a == 0:
@@ -396,40 +433,38 @@
             q[a * N, rows, :] -= float(PEN * WEIGHTS[a]) * edge[0, a]
             q[a * N + N - 1, rows, :] -= float(PEN * WEIGHTS[a]) * edge[1, a]
 
-    def arrive_second(c):
-        def row(a, carry):
-            for h in range(ZL // 8):
-                rows = [fbuf[c, s, a, pl.ds(h * 8, 8), :] for s in range(NP)]
-                for b, line in enumerate(block_transpose(rows)):
-                    res[a * N + b, pl.ds(pl.multiple_of(c * ZL + h * 8, 8), 8), :] = line
+    def arrive_second(c, pair):
+        for i in range(NP - 1):
+            copy2(c, pair, i).wait_recv()
+        for k in (0, 1):
+            a = 2 * pair + k
+            lines = block_transpose([fbuf[c, s, a] for s in range(NP)])
+            for b, line in enumerate(lines):
+                res[a * N + b, sys_rows(c), :] = line
+
+    def begin(c):
+        def pair(k, carry):
+            arrive_second(c, k)
+            send_r_edges(c, k)
             return carry
 
-        def pair(k, carry):
-            for i in range(NP - 1):
-                copy2(c, k, i).wait_recv()
-            return lax.fori_loop(2 * k, 2 * k + 2, row, carry)
-
         lax.fori_loop(0, PAIRS, pair, 0)
-
-    def begin(c):
-        arrive_second(c)
-        send_edges(res, c, 0)
-        apply_local(res, qv, c)
-        send_edges(qv, c, 1)
+        take_faces(res, c)
+        apply_local(res, qv, c, (0,))
+        send_q_edges(c)
+        apply_local(res, qv, c, (1, 2, 3))
 
     def end(c):
-        take_edges(c, 0)
+        def wait_r(k, carry):
+            for way in (0, 1):
+                r_halo(c, way, k).wait_recv()
+            return carry
+
+        lax.fori_loop(0, PAIRS, wait_r, 0)
+        take_edges(rrecv, c)
         add_edges(qv, c)
-        apply_local(qv, pv, c)
-        take_edges(c, 1)
-        rows = sys_rows(c)
-        inner = jnp.broadcast_to(lid < 64, (ZL, ED)) & (e > 0)
-        outer = jnp.broadcast_to(lid >= 64, (ZL, ED)) & (e < NE - 1)
-        for a in range(N):
-            w_a = float(PEN * WEIGHTS[a])
-            edge[0, a] -= jnp.where(inner, w_a * res[a * N, rows, :], 0.0)
-            edge[1, a] -= jnp.where(outer, w_a * res[a * N + N - 1, rows, :], 0.0)
-        add_edges(pv, c)
+        take_faces(qv, c)
+        apply_local(qv, pv, c, range(N // 2))
 
         def dot_tile(h, carry):
             rows = pl.ds(pl.multiple_of(c * ZL + h * 8, 8), 8)
@@ -443,6 +478,21 @@
             return carry
 
         lax.fori_loop(0, ZL // 8, dot_tile, 0)
+        for way in (0, 1):
+            q_halo(c, way).wait_recv()
+        take_edges(qrecv, c)
+        rows = sys_rows(c)
+        inner = jnp.broadcast_to(lid < 64, (ZL, ED)) & (e > 0)
+        outer = jnp.broadcast_to(lid >= 64, (ZL, ED)) & (e < NE - 1)
+        last = jnp.zeros((ZL, ED), F32)
+        for a in range(N):
+            w_a = float(PEN * WEIGHTS[a])
+            for way, b, where in ((0, 0, inner), (1, N - 1, outer)):
+                n = a * N + b
+                got = w_a * (edge[way, a] - jnp.where(where, w_a * res[n, rows, :], 0.0))
+                pv[n, rows, :] -= got
+                last = last + qv[n, rows, :] * got
+        dots[3, rows, :] -= last
 
     begin(0)
 
@@ -509,9 +559,10 @@
         return carry
 
     def drain3(c, carry):
-        for kind in (0, 1):
-            for way in (0, 1):
-                halo(c, kind, way).wait_send()
+        for way in (0, 1):
+            for pair in range(PAIRS):
+                r_halo(c, way, pair).wait_send()
+            q_halo(c, way).wait_send()
         return carry
 
     lax.fori_loop(0, N, drain, 0)
@@ -525,10 +576,16 @@
     def tile(st, carry):
         rows = pl.ds(pl.multiple_of(st * 8, 8), 8)
         s, t = coef[0, rows, :], coef[1, rows, :]
-        for n in range(N * N):
-            r_n, q_n, p_n = r[n, rows, :], q[n, rows, :], p[n, rows, :]
-            xs[st, pl.ds(n, 8, stride=N * N), :] = s * r_n - t * q_n
-            rs[st, pl.ds(n, 8, stride=N * N), :] = r_n - s * q_n + t * p_n
+        for a in range(N):
+            new, left = [], []
+            for n in range(a * N, a * N + N):
+                r_n, q_n, p_n = r[n, rows, :], q[n, rows, :], p[n, rows, :]
+                new.append(s * r_n - t * q_n)
+                left.append(r_n - s * q_n + t * p_n)
+            for buf, vals in ((xs, new), (rs, left)):
+                vals = jnp.swapaxes(jnp.stack(vals), 0, 1)
+                for k in range(8):
+                    buf[st, pl.ds(k * N * N + a * N, N), :] = vals[k]
         for copy in out_copies(st):
             copy.start()
         return carry
@@ -549,7 +606,7 @@
 
 
 def on_device(velocity, elem_scale, elem_ids, edge_blocks):
-    vel = velocity.reshape(SYS * N * N, ED)
+    vel = velocity.reshape(SYS, N * N, ED)
     rows = np.zeros((ROWS, ED))
     rows[: N * N] = (-WEIGHTS[:, None] * DERIV).T.reshape(N * N, 1)
     rows[ROW_W : ROW_W + N] = WEIGHTS[:, None]
@@ -568,7 +625,7 @@
         in_specs=[hbm] * 5,
         out_specs=(vmem,) * 4,
         scratch_shapes=[
-            pltpu.VMEM((SYS * N * N, ED), F32),
+            pltpu.VMEM((SYS, N * N, ED), F32),
             pltpu.VMEM((2, ED), F32),
             pltpu.VMEM((1, ED), jnp.int32),
             pltpu.VMEM((ROWS, ED), F32),
@@ -584,8 +641,10 @@
             pltpu.VMEM((12, ED, ED), BF16),
             pltpu.VMEM((4, N, ZL, ED), F32),
             pltpu.VMEM((2, N, ZL, ED), F32),
-            pltpu.VMEM((3, 2, 2, N // 2, ZL, ED), F32),
-            pltpu.VMEM((3, 2, 2, N // 2, ZL, ED), F32),
+            pltpu.VMEM((3, 2, PAIRS, ZL, ED), F32),
+            pltpu.VMEM((3, 2, PAIRS, ZL, ED), F32),
+            pltpu.VMEM((3, 2, PAIRS, ZL, ED), F32),
+            pltpu.VMEM((3, 2, PAIRS, ZL, ED), F32),
             pltpu.VMEM((4, ED, ED), F32),
             pltpu.VMEM((NE, 8, ED), F32),
             dma((5,)),
@@ -593,8 +652,10 @@
             dma((N, NP - 1)),
             dma((3, PAIRS, NP - 1)),
             dma((3, PAIRS, NP - 1)),
-            dma((3, 2, 2)),
-            dma((3, 2, 2)),
+            dma((3, 2, PAIRS)),
+            dma((3, 2, PAIRS)),
+            dma((3, 2)),
+            dma((3, 2)),
             dma((NE - 1,)),
             dma((NE - 1,)),
         ],

time: 69.7 us -> 67.4 us (0.967)
  Pallas kernels: 68.2 us -> 66.1 us
    pallas_call x1, Pallas kernels: 65.3 us -> 64.3 us  [on_device(): pl.pallas_call(kernel, out_shape=(field, field, field, jax.ShapeDtypeStru...]
    pallas_call x1, Pallas kernels: 2.88 us -> 1.83 us  [on_device(): pl.pallas_call(finish_kernel, out_shape=(flat, flat), in_specs=[vmem] * 4...]
where the time goes in v3:
time: 67.4 us; the launch traced here: 66.8 us
  Pallas kernels  66.1 us (98%)
    pallas_call x1, Pallas kernels, on_device(): pl.pallas_call(kernel, out_shape=(field, field, field, jax.ShapeDtypeStru...  64.3 us
    pallas_call x1, Pallas kernels, on_device(): pl.pallas_call(finish_kernel, out_shape=(flat, flat), in_specs=[vmem] * 4...  1.83 us

profile of v3, /device:TPU:2, one launch (start us, length us, event | category | flops | bytes accessed | tf_op | source)
XLA Modules:
  0.0 66.8 jit_solution(16291638968282263720)
XLA Ops:
  0.6 64.3 %exchange_and_apply.1 = (f32[64,48,128]{2,1,0:T(8,128)S(1)}, f32[64,48,128]{2,1,0:T(8,128)S(1)}, f32[64,48,128]{2,1,0:T(8,128)S(1)}, f32[2,48,128]{2,1,0:T(8,128)S(1)}) custom-call(f32[48,64,128]{2,1,0:T(8,128)} %bitcast.3, f32[2,128]{1,0:T(2,128)} %scale_in.1, s32[1,128]{1,0:T(1,128)} %ids_in.1, f32[80,128]{1,0:T(8,128)} %constant.4.clone.rows_in, ...), custom_call_target="tpu_custom_call" | custom-call | tf_op jit(solution)/shard_map/exchange_and_apply/pallas_call | solution.py:622
  64.9 1.8 %finish.1 = (f32[6,512,128]{2,1,0:T(8,128)}, f32[6,512,128]{2,1,0:T(8,128)}) custom-call(f32[64,48,128]{2,1,0:T(8,128)S(1)} %get-tuple-element.8.r, f32[64,48,128]{2,1,0:T(8,128)S(1)} %get-tuple-element.9.q, f32[64,48,128]{2,1,0:T(8,128)S(1)} %get-tuple-element.10.p, f32[2,48,128]{2,1,0:T(8,128)S(1)} %get-tuple-element.11.coef), custom_call_target="tpu_custom_call" | custom-call | tf_op jit(solution)/shard_map/finish/pallas_call | solution.py:669

commit v4 on v3

--- a/solution.py
+++ b/solution.py
@@ -19,16 +19,17 @@
 Z = 128
 NP = 8
 ZL = Z // NP
-EG = ED // NP
+HALVES = 2
+GROUPS = NP * HALVES
+EG = ED // GROUPS
+AH = N // 2
 SYS = 3 * ZL
 NX = 4
 NZ = 8
 NE = NX * NZ
-PAIRS = N // 2
 PEN = 8.0
-ROW_W = N * N
-ROW_LANE = ROW_W + N
-ROWS = 80
+ROW_SAME, ROW_SWAP, ROW_AB, ROW_B = 0, AH * AH, 2 * AH * AH, 2 * AH * AH + AH
+ROWS = 40
 LAM = 4.0
 STEP = 0.1
 
@@ -96,15 +97,17 @@
 
 def block_transpose(rows):
     rows = list(rows)
-    lane = lax.broadcasted_iota(jnp.int32, rows[0].shape, rows[0].ndim - 1) // EG
-    for d in (1, 2, 4):
+    axis = rows[0].ndim - 1
+    lane = lax.broadcasted_iota(jnp.int32, rows[0].shape, axis) // EG
+    d = 1
+    while d < GROUPS:
         clear = (lane & d) == 0
-        for i in range(NP):
+        for i in range(GROUPS):
             if i & d == 0:
                 x, y = rows[i], rows[i + d]
-                axis = x.ndim - 1
                 rows[i] = jnp.where(clear, x, pltpu.roll(y, EG * d, axis))
                 rows[i + d] = jnp.where(clear, pltpu.roll(x, ED - EG * d, axis), y)
+        d *= 2
     return rows
 
 
@@ -144,6 +147,7 @@
     fsend,
     fbuf,
     geo,
+    part_geo,
     hel,
     tables,
     face,
@@ -200,66 +204,72 @@
     geo[0:1, :] = circ * radial
     geo[1:2, :] = radial / circ
     geo[2:3, :] = circ / radial
-    lane_row = lax.broadcasted_iota(jnp.int32, (1, ED), 1)
-    for k, val in ((3, circ), (4, radial)):
-        val = pltpu.roll(jnp.broadcast_to(val, (8, ED)), lax.rem(ED - EG * me, ED), 1)
-        val = jnp.where(lax.broadcasted_iota(jnp.int32, (8, ED), 1) < EG, val, 0.0)
-        for d in (1, 2, 4):
-            val = val + pltpu.roll(val, EG * d, 1)
-        geo[k : k + 1, :] = val[0:1, :]
-    wl = ctab[ROW_LANE : ROW_LANE + 1, :]
-    g_circ, g_radial = geo[3:4, :], geo[4:5, :]
-    geo[5:6, :] = g_circ * g_radial * wl
-    geo[6:7, :] = g_circ * wl
-    geo[7:8, :] = g_radial * wl
-
-    def copy1(a, i):
+    for half in range(HALVES):
+        share = []
+        for val in (circ, radial):
+            first = ED - EG * (HALVES * me + half)
+            val = pltpu.roll(jnp.broadcast_to(val, (8, ED)), lax.rem(first, ED), 1)
+            val = jnp.where(lax.broadcasted_iota(jnp.int32, (8, ED), 1) < EG, val, 0.0)
+            for d in (1, 2, 4, 8):
+                val = val + pltpu.roll(val, EG * d, 1)
+            share.append(val[0:1, :])
+        g_circ, g_radial = share
+        part_geo[half, 0:1, :] = g_circ * g_radial
+        part_geo[half, 1:2, :] = g_circ
+        part_geo[half, 2:3, :] = g_radial * ctab[ROW_B : ROW_B + 1, :]
+
+    def copy1(half, ah, i):
         t = plane_peers[i]
         return pltpu.make_async_remote_copy(
-            src_ref=xsend.at[a, t],
-            dst_ref=xbuf.at[a, :, pl.ds(pl.multiple_of(me * ZL, ZL), ZL), :],
-            send_sem=s1.at[a, i],
-            recv_sem=r1.at[a, i],
+            src_ref=xsend.at[half, ah, t],
+            dst_ref=xbuf.at[half, ah, :, pl.ds(pl.multiple_of(me * ZL, ZL), ZL), :],
+            send_sem=s1.at[half, ah, i],
+            recv_sem=r1.at[half, ah, i],
             device_id=(e, t),
             device_id_type=MESH,
         )
 
-    def copy2(c, pair, i):
+    def copy2(half, c, k, i):
         t = plane_peers[i]
         return pltpu.make_async_remote_copy(
-            src_ref=fsend.at[c, pl.ds(2 * pair, 2), pl.ds(pl.multiple_of(t * ZL, ZL), ZL), :],
-            dst_ref=fbuf.at[c, me, pl.ds(2 * pair, 2)],
-            send_sem=s2.at[c, pair, i],
-            recv_sem=r2.at[c, pair, i],
+            src_ref=fsend.at[half, c, pl.ds(2 * k, 2), pl.ds(pl.multiple_of(t * ZL, ZL), ZL), :],
+            dst_ref=fbuf.at[half, c, me, pl.ds(2 * k, 2)],
+            send_sem=s2.at[half, c, k, i],
+            recv_sem=r2.at[half, c, k, i],
             device_id=(e, t),
             device_id_type=MESH,
         )
 
-    def pack_first(a):
+    def pack_first(ah):
         for c in range(3):
-            for h in range(ZL // 8):
-                tile = vin[pl.ds(c * ZL + h * 8, 8), pl.ds(pl.multiple_of(a * N, N), N), :]
-                tile = jnp.swapaxes(tile, 0, 1)
-                for q, row in enumerate(block_transpose([tile[b] for b in range(N)])):
-                    xsend[a, q, c, pl.ds(h * 8, 8), :] = row
-
-    def send_first(a):
+            for z8 in range(ZL // 8):
+                nodes = pl.ds(pl.multiple_of(ah * 2 * N, 2 * N), 2 * N)
+                tile = jnp.swapaxes(vin[pl.ds(c * ZL + z8 * 8, 8), nodes, :], 0, 1)
+                for g, row in enumerate(block_transpose([tile[k] for k in range(2 * N)])):
+                    xsend[g % HALVES, ah, g // HALVES, c, pl.ds(z8 * 8, 8), :] = row
+
+    def send_first(half, ah):
         for i in range(NP - 1):
-            copy1(a, i).start()
+            copy1(half, ah, i).start()
         mine = pl.ds(pl.multiple_of(me * ZL, ZL), ZL)
-        xbuf[a, :, mine, :] = xsend[a, me]
+        xbuf[half, ah, :, mine, :] = xsend[half, ah, me]
 
     loads[0].wait()
     pack_first(0)
     pl.semaphore_wait(barrier, NP - 1 + NE - 1)
-    send_first(0)
-
-    def first(a, carry):
-        pack_first(a)
-        send_first(a)
-        return carry
-
-    lax.fori_loop(1, N, first, 0)
+    send_first(0, 0)
+
+    def first(ah, carry):
+        pack_first(ah)
+        send_first(0, ah)
+        return carry
+
+    def first_rest(ah, carry):
+        send_first(1, ah)
+        return carry
+
+    lax.fori_loop(1, AH, first, 0)
+    lax.fori_loop(0, AH, first_rest, 0)
 
     acc[...] = jnp.zeros_like(acc)
     dots[...] = jnp.zeros_like(dots)
@@ -287,47 +297,53 @@
     kappa = jnp.where(slot == 1, Z // 2, slot // 2).astype(F32)
     hel[...] = (LAM + (STEP * kappa) * (STEP * kappa)) * geo[0:1, :]
 
-    def arrive_first(p, carry):
-        for i in range(NP - 1):
-            copy1(p, i).wait_recv()
-        w_p = ctab[pl.ds(ROW_W + p, 1), :]
-        mass = geo[5:6, :] * w_p
-        g_y = geo[6:7, :] * w_p
-        g_x = geo[7:8, :]
-        for c in range(3):
-            fy_high, fy_low = split(xbuf[p, 1] * xbuf[p, c])
-            dy = dot(fy_high, mats[4]) + dot(fy_low, mats[4]) + dot(fy_high, mats[5])
-            acc[p, c] += (LAM * mass) * xbuf[p, c] - g_y * dy
-            b_high, b_low = split(mass * (xbuf[p, 2] * xbuf[p, c]))
-            bbuf[p, 0, c] = b_high
-            bbuf[p, 1, c] = b_low
-            for h in range(4):
-                rows = pl.ds(h * 32, 32)
-                fx = g_x * (xbuf[p, 0, rows, :] * xbuf[p, c, rows, :])
-                for a in range(N):
-                    acc[a, c, rows, :] += ctab[pl.ds(p * N + a, 1), :] * fx
-        return carry
-
-    lax.fori_loop(0, N, arrive_first, 0)
-
     f_high = jnp.concatenate([mats[0], mats[1]], axis=1)
     f_low = jnp.concatenate([mats[2], mats[3]], axis=1)
 
-    def send_second(step, carry):
-        c, pair = step // PAIRS, lax.rem(step, PAIRS)
-        for k in (0, 1):
-            a = 2 * pair + k
-            a_high, a_low = split(acc[a, c])
-            high = jnp.concatenate([a_high, bbuf[a, 0, c]], axis=0)
-            low = jnp.concatenate([a_low, bbuf[a, 1, c]], axis=0)
-            fsend[c, a] = dot(f_high, high) + dot(f_high, low) + dot(f_low, high)
-        for i in range(NP - 1):
-            copy2(c, pair, i).start()
-        mine = pl.ds(pl.multiple_of(me * ZL, ZL), ZL)
-        fbuf[c, me, pl.ds(2 * pair, 2)] = fsend[c, pl.ds(2 * pair, 2), mine, :]
-        return carry
-
-    lax.fori_loop(0, 3 * PAIRS, send_second, 0)
+    def between(half, carry):
+        def arrive_first(ph, carry):
+            for i in range(NP - 1):
+                copy1(half, ph, i).wait_recv()
+            w_ab = ctab[pl.ds(ROW_AB + ph, 1), :]
+            mass = part_geo[half, 0:1, :] * w_ab
+            g_y = part_geo[half, 1:2, :] * w_ab
+            g_x = part_geo[half, 2:3, :]
+            for c in range(3):
+                fy_high, fy_low = split(xbuf[half, ph, 1] * xbuf[half, ph, c])
+                dy = dot(fy_high, mats[4]) + dot(fy_low, mats[4]) + dot(fy_high, mats[5])
+                acc[half, ph, c] += (LAM * mass) * xbuf[half, ph, c] - g_y * dy
+                b_high, b_low = split(mass * (xbuf[half, ph, 2] * xbuf[half, ph, c]))
+                bbuf[half, ph, 0, c] = b_high
+                bbuf[half, ph, 1, c] = b_low
+                for k in range(4):
+                    rows = pl.ds(k * 32, 32)
+                    fx = g_x * (xbuf[half, ph, 0, rows, :] * xbuf[half, ph, c, rows, :])
+                    swap = pltpu.roll(fx, ED // 2, 1)
+                    for ah in range(AH):
+                        same = ctab[pl.ds(ROW_SAME + ph * AH + ah, 1), :]
+                        other = ctab[pl.ds(ROW_SWAP + ph * AH + ah, 1), :]
+                        acc[half, ah, c, rows, :] += same * fx + other * swap
+            return carry
+
+        def send_second(step, carry):
+            c, k = step // 2, lax.rem(step, 2)
+            for j in (0, 1):
+                ah = 2 * k + j
+                a_high, a_low = split(acc[half, ah, c])
+                high = jnp.concatenate([a_high, bbuf[half, ah, 0, c]], axis=0)
+                low = jnp.concatenate([a_low, bbuf[half, ah, 1, c]], axis=0)
+                fsend[half, c, ah] = dot(f_high, high) + dot(f_high, low) + dot(f_low, high)
+            for i in range(NP - 1):
+                copy2(half, c, k, i).start()
+            mine = pl.ds(pl.multiple_of(me * ZL, ZL), ZL)
+            fbuf[half, c, me, pl.ds(2 * k, 2)] = fsend[half, c, pl.ds(2 * k, 2), mine, :]
+            return carry
+
+        lax.fori_loop(0, AH, arrive_first, 0)
+        lax.fori_loop(0, 6, send_second, 0)
+        return carry
+
+    lax.fori_loop(0, HALVES, between, 0)
 
     def sys_rows(c):
         return pl.ds(pl.multiple_of(c * ZL, ZL), ZL)
@@ -371,18 +387,18 @@
             r_halo(c, way, pair).start()
 
     def send_q_edges(c):
-        for way, got in enumerate(pack_edges(qv, c, 0, PAIRS)):
-            qsend[c, way] = got.reshape(PAIRS, ZL, ED)
+        for way, got in enumerate(pack_edges(qv, c, 0, AH)):
+            qsend[c, way] = got.reshape(AH, ZL, ED)
             q_halo(c, way).start()
 
     def take_edges(recv, c):
         for way in (0, 1):
             there = (e > 0) if way == 0 else (e < NE - 1)
-            got = recv[c, way].reshape(PAIRS * ZL, ED)
+            got = recv[c, way].reshape(AH * ZL, ED)
             for k in (0, 1):
                 here = jnp.where(there, pick(got, tables[8 + 2 * way + k]), 0.0)
-                here = here.reshape(PAIRS, ZL, ED)
-                for pair in range(PAIRS):
+                here = here.reshape(AH, ZL, ED)
+                for pair in range(AH):
                     edge[way, 2 * pair + k] = here[pair]
 
     def take_faces(v, c):
@@ -433,22 +449,27 @@
             q[a * N, rows, :] -= float(PEN * WEIGHTS[a]) * edge[0, a]
             q[a * N + N - 1, rows, :] -= float(PEN * WEIGHTS[a]) * edge[1, a]
 
-    def arrive_second(c, pair):
-        for i in range(NP - 1):
-            copy2(c, pair, i).wait_recv()
-        for k in (0, 1):
-            a = 2 * pair + k
-            lines = block_transpose([fbuf[c, s, a] for s in range(NP)])
-            for b, line in enumerate(lines):
-                res[a * N + b, sys_rows(c), :] = line
+    def arrive_second(c, ah):
+        groups = [fbuf[g % HALVES, c, g // HALVES, ah] for g in range(GROUPS)]
+        for k, line in enumerate(block_transpose(groups)):
+            res[ah * 2 * N + k, sys_rows(c), :] = line
+
+    def dot_rows(first, k, count):
+        return pl.ds(pl.multiple_of(first + (k % 2) * (ED // 2), 8), count)
 
     def begin(c):
-        def pair(k, carry):
-            arrive_second(c, k)
-            send_r_edges(c, k)
+        def arrive(ah, carry):
+            arrive_second(c, ah)
+            send_r_edges(c, ah)
             return carry
 
-        lax.fori_loop(0, PAIRS, pair, 0)
+        def arrive_pair(k, carry):
+            for half in range(HALVES):
+                for i in range(NP - 1):
+                    copy2(half, c, k, i).wait_recv()
+            return lax.fori_loop(2 * k, 2 * k + 2, arrive, carry)
+
+        lax.fori_loop(0, 2, arrive_pair, 0)
         take_faces(res, c)
         apply_local(res, qv, c, (0,))
         send_q_edges(c)
@@ -460,7 +481,7 @@
                 r_halo(c, way, k).wait_recv()
             return carry
 
-        lax.fori_loop(0, PAIRS, wait_r, 0)
+        lax.fori_loop(0, AH, wait_r, 0)
         take_edges(rrecv, c)
         add_edges(qv, c)
         take_faces(qv, c)
@@ -474,7 +495,7 @@
                 for k, prod in enumerate((r_n * r_n, r_n * q_n, q_n * q_n, q_n * p_n)):
                     sums[k] = sums[k] + prod
             for k in range(4):
-                dots[k, rows, :] = sums[k]
+                dots[k // 2, dot_rows(c * ZL + h * 8, k, 8), :] = sums[k]
             return carry
 
         lax.fori_loop(0, ZL // 8, dot_tile, 0)
@@ -492,22 +513,21 @@
                 got = w_a * (edge[way, a] - jnp.where(where, w_a * res[n, rows, :], 0.0))
                 pv[n, rows, :] -= got
                 last = last + qv[n, rows, :] * got
-        dots[3, rows, :] -= last
-
-    begin(0)
-
-    def component(c, carry):
+        dots[1, dot_rows(c * ZL, 3, ZL), :] -= last
+
+    def begin_all(c, carry):
         begin(c)
-        end(c - 1)
-        return carry
-
-    lax.fori_loop(1, 3, component, 0)
-    end(2)
+        return carry
+
+    def end_all(c, carry):
+        end(c)
+        return carry
+
+    lax.fori_loop(0, 3, begin_all, 0)
+    lax.fori_loop(0, 3, end_all, 0)
 
     one_rows = jnp.ones((8, ED), F32)
-    row8 = lax.broadcasted_iota(jnp.int32, (8, ED), 0)
-    part = jnp.zeros((8, ED), F32)
-    for k in range(4):
+    for k in (0, 1):
         summed = lax.dot_general(
             one_rows,
             dots[k],
@@ -515,9 +535,7 @@
             precision=lax.Precision.HIGHEST,
             preferred_element_type=F32,
         )
-        part = jnp.where(row8 == k, summed, part)
-
-    rbuf[0] = part
+        rbuf[0, k : k + 1, :] = summed[0:1, :]
 
     def spread(i):
         return pltpu.make_async_remote_copy(
@@ -535,38 +553,42 @@
         spread(i).wait_recv()
     part = jnp.sum(rbuf[...], axis=0)
 
-    aa, bb, cc, ee = (part[k : k + 1, :] for k in range(4))
+    swapped = pltpu.roll(jnp.concatenate([part] * 4, axis=0), ED // 2, 1)
+    aa, bb, cc, ee = part[0:1, :], swapped[0:1, :], part[1:2, :], swapped[1:2, :]
     alpha = aa / bb
     rr1 = alpha * alpha * cc - aa
     beta1 = 1.0 + rr1 / aa
     alpha1 = rr1 / (beta1 * beta1 * bb - 2.0 * beta1 * alpha * cc + alpha * alpha * ee)
     coef_s = alpha + alpha1 * beta1
     coef_t = alpha1 * alpha
+    row8 = lax.broadcasted_iota(jnp.int32, (8, ED), 0)
     both = jnp.where(row8 == 0, coef_s, coef_t)
     both = jnp.where(lax.broadcasted_iota(jnp.int32, (8, ED), 1) < SYS, both, 0.0)
     both = jnp.transpose(jnp.concatenate([both] + [jnp.zeros((8, ED), F32)] * 15, axis=0))
     coef_out[0] = jnp.broadcast_to(both[0:SYS, 0:1], (SYS, ED))
     coef_out[1] = jnp.broadcast_to(both[0:SYS, 1:2], (SYS, ED))
 
-    def drain(a, carry):
-        for i in range(NP - 1):
-            copy1(a, i).wait_send()
+    def drain(ah, carry):
+        for half in range(HALVES):
+            for i in range(NP - 1):
+                copy1(half, ah, i).wait_send()
         return carry
 
     def drain2(step, carry):
-        for i in range(NP - 1):
-            copy2(step // PAIRS, lax.rem(step, PAIRS), i).wait_send()
+        for half in range(HALVES):
+            for i in range(NP - 1):
+                copy2(half, step // 2, lax.rem(step, 2), i).wait_send()
         return carry
 
     def drain3(c, carry):
         for way in (0, 1):
-            for pair in range(PAIRS):
+            for pair in range(AH):
                 r_halo(c, way, pair).wait_send()
             q_halo(c, way).wait_send()
         return carry
 
-    lax.fori_loop(0, N, drain, 0)
-    lax.fori_loop(0, 3 * PAIRS, drain2, 0)
+    lax.fori_loop(0, AH, drain, 0)
+    lax.fori_loop(0, 6, drain2, 0)
     lax.fori_loop(0, 3, drain3, 0)
     for i in range(NE - 1):
         spread(i).wait_send()
@@ -608,12 +630,19 @@
 def on_device(velocity, elem_scale, elem_ids, edge_blocks):
     vel = velocity.reshape(SYS, N * N, ED)
     rows = np.zeros((ROWS, ED))
-    rows[: N * N] = (-WEIGHTS[:, None] * DERIV).T.reshape(N * N, 1)
-    rows[ROW_W : ROW_W + N] = WEIGHTS[:, None]
-    rows[ROW_LANE] = np.repeat(WEIGHTS, EG)
+    table = -WEIGHTS[:, None] * DERIV
+    for ph in range(AH):
+        for ah in range(AH):
+            for i in (0, 1):
+                lanes = slice(i * ED // 2, (i + 1) * ED // 2)
+                rows[ROW_SAME + ph * AH + ah, lanes] = table[2 * ah + i, 2 * ph + i]
+                rows[ROW_SWAP + ph * AH + ah, lanes] = table[2 * ah + i, 2 * ph + 1 - i]
+    for ah in range(AH):
+        rows[ROW_AB + ah] = np.repeat(np.outer(WEIGHTS[2 * ah : 2 * ah + 2], WEIGHTS).ravel(), EG)
+    rows[ROW_B] = np.repeat(np.tile(WEIGHTS, 2), EG)
     rows = jnp.asarray(rows, F32)
     four = halves(mode_matrix()).reshape(2, Z, 2, Z).transpose(0, 2, 1, 3).reshape(4, Z, Z)
-    mats = jnp.asarray(np.concatenate([four, halves(np.kron(DERIV.T, np.eye(EG)))]))
+    mats = jnp.asarray(np.concatenate([four, halves(np.kron(np.eye(2), np.kron(DERIV.T, np.eye(EG))))]))
     operands = (vel, elem_scale, elem_ids, rows, mats)
     vmem = pl.BlockSpec(memory_space=pltpu.VMEM)
     hbm = pl.BlockSpec(memory_space=pltpu.HBM)
@@ -630,30 +659,31 @@
             pltpu.VMEM((1, ED), jnp.int32),
             pltpu.VMEM((ROWS, ED), F32),
             pltpu.VMEM((6, ED, ED), BF16),
-            pltpu.VMEM((N, NP, 3, ZL, ED), F32),
-            pltpu.VMEM((N, 3, Z, ED), F32),
-            pltpu.VMEM((N, 3, Z, ED), F32),
-            pltpu.VMEM((N, 2, 3, Z, ED), BF16),
-            pltpu.VMEM((3, N, Z, ED), F32),
-            pltpu.VMEM((3, NP, N, ZL, ED), F32),
+            pltpu.VMEM((HALVES, AH, NP, 3, ZL, ED), F32),
+            pltpu.VMEM((HALVES, AH, 3, Z, ED), F32),
+            pltpu.VMEM((HALVES, AH, 3, Z, ED), F32),
+            pltpu.VMEM((HALVES, AH, 2, 3, Z, ED), BF16),
+            pltpu.VMEM((HALVES, 3, AH, Z, ED), F32),
+            pltpu.VMEM((HALVES, 3, NP, AH, ZL, ED), F32),
             pltpu.VMEM((8, ED), F32),
+            pltpu.VMEM((HALVES, 8, ED), F32),
             pltpu.VMEM((SYS, ED), F32),
             pltpu.VMEM((12, ED, ED), BF16),
             pltpu.VMEM((4, N, ZL, ED), F32),
             pltpu.VMEM((2, N, ZL, ED), F32),
-            pltpu.VMEM((3, 2, PAIRS, ZL, ED), F32),
-            pltpu.VMEM((3, 2, PAIRS, ZL, ED), F32),
-            pltpu.VMEM((3, 2, PAIRS, ZL, ED), F32),
-            pltpu.VMEM((3, 2, PAIRS, ZL, ED), F32),
-            pltpu.VMEM((4, ED, ED), F32),
-            pltpu.VMEM((NE, 8, ED), F32),
+            pltpu.VMEM((3, 2, AH, ZL, ED), F32),
+            pltpu.VMEM((3, 2, AH, ZL, ED), F32),
+            pltpu.VMEM((3, 2, AH, ZL, ED), F32),
+            pltpu.VMEM((3, 2, AH, ZL, ED), F32),
+            pltpu.VMEM((2, ED, ED), F32),
+            pltpu.VMEM((NE, 2, ED), F32),
             dma((5,)),
-            dma((N, NP - 1)),
-            dma((N, NP - 1)),
-            dma((3, PAIRS, NP - 1)),
-            dma((3, PAIRS, NP - 1)),
-            dma((3, 2, PAIRS)),
-            dma((3, 2, PAIRS)),
+            dma((HALVES, AH, NP - 1)),
+            dma((HALVES, AH, NP - 1)),
+            dma((HALVES, 3, 2, NP - 1)),
+            dma((HALVES, 3, 2, NP - 1)),
+            dma((3, 2, AH)),
+            dma((3, 2, AH)),
             dma((3, 2)),
             dma((3, 2)),
             dma((NE - 1,)),

time: 67.4 us -> 67.2 us (level)
  no operation moved by 1% of the time
where the time goes in v4:
time: 67.2 us; the launch traced here: 66.3 us
  Pallas kernels  65.7 us (98%)
    pallas_call x1, Pallas kernels, on_device(): pl.pallas_call(kernel, out_shape=(field, field, field, jax.ShapeDtypeStru...  63.8 us
    pallas_call x1, Pallas kernels, on_device(): pl.pallas_call(finish_kernel, out_shape=(flat, flat), in_specs=[vmem] * 4...  1.83 us

profile of v4, /device:TPU:2, one launch (start us, length us, event | category | flops | bytes accessed | tf_op | source)
XLA Modules:
  0.0 66.3 jit_solution(7912824912200612265)
XLA Ops:
  0.6 63.8 %exchange_and_apply.1 = (f32[64,48,128]{2,1,0:T(8,128)S(1)}, f32[64,48,128]{2,1,0:T(8,128)S(1)}, f32[64,48,128]{2,1,0:T(8,128)S(1)}, f32[2,48,128]{2,1,0:T(8,128)S(1)}) custom-call(f32[48,64,128]{2,1,0:T(8,128)} %bitcast.3, f32[2,128]{1,0:T(2,128)} %scale_in.1, s32[1,128]{1,0:T(1,128)} %ids_in.1, f32[40,128]{1,0:T(8,128)} %constant.4.clone.rows_in, ...), custom_call_target="tpu_custom_call" | custom-call | tf_op jit(solution)/shard_map/exchange_and_apply/pallas_call | solution.py:651
  64.5 1.8 %finish.1 = (f32[6,512,128]{2,1,0:T(8,128)}, f32[6,512,128]{2,1,0:T(8,128)}) custom-call(f32[64,48,128]{2,1,0:T(8,128)S(1)} %get-tuple-element.8.r, f32[64,48,128]{2,1,0:T(8,128)S(1)} %get-tuple-element.9.q, f32[64,48,128]{2,1,0:T(8,128)S(1)} %get-tuple-element.10.p, f32[2,48,128]{2,1,0:T(8,128)S(1)} %get-tuple-element.11.coef), custom_call_target="tpu_custom_call" | custom-call | tf_op jit(solution)/shard_map/finish/pallas_call | solution.py:699

commit v5 on v4

--- a/solution.py
+++ b/solution.py
@@ -95,20 +95,21 @@
     return dot(high, table) + dot(low, table)
 
 
-def block_transpose(rows):
-    rows = list(rows)
-    axis = rows[0].ndim - 1
-    lane = lax.broadcasted_iota(jnp.int32, rows[0].shape, axis) // EG
+def turned(x, groups):
+    shift = EG * (groups % GROUPS)
+    return pltpu.roll(x, shift, x.ndim - 1) if shift else x
+
+
+def block_transpose(rows, turned_before=False):
+    if not turned_before:
+        rows = [turned(x, i) for i, x in enumerate(rows)]
+    lane = lax.broadcasted_iota(jnp.int32, rows[0].shape, rows[0].ndim - 1) // EG
     d = 1
     while d < GROUPS:
         clear = (lane & d) == 0
-        for i in range(GROUPS):
-            if i & d == 0:
-                x, y = rows[i], rows[i + d]
-                rows[i] = jnp.where(clear, x, pltpu.roll(y, EG * d, axis))
-                rows[i + d] = jnp.where(clear, pltpu.roll(x, ED - EG * d, axis), y)
+        rows = [jnp.where(clear, rows[i], rows[(i + d) % GROUPS]) for i in range(GROUPS)]
         d *= 2
-    return rows
+    return [turned(rows[-g % GROUPS], -g) for g in range(GROUPS)]
 
 
 def stiff_times(v, wanted):
@@ -332,7 +333,8 @@
                 a_high, a_low = split(acc[half, ah, c])
                 high = jnp.concatenate([a_high, bbuf[half, ah, 0, c]], axis=0)
                 low = jnp.concatenate([a_low, bbuf[half, ah, 1, c]], axis=0)
-                fsend[half, c, ah] = dot(f_high, high) + dot(f_high, low) + dot(f_low, high)
+                out = dot(f_high, high) + dot(f_high, low) + dot(f_low, high)
+                fsend[half, c, ah] = pltpu.roll(out, EG * (HALVES * me + half), 1)
             for i in range(NP - 1):
                 copy2(half, c, k, i).start()
             mine = pl.ds(pl.multiple_of(me * ZL, ZL), ZL)
@@ -348,12 +350,12 @@
     def sys_rows(c):
         return pl.ds(pl.multiple_of(c * ZL, ZL), ZL)
 
-    def r_halo(c, way, pair):
+    def r_halo(c, way):
         return pltpu.make_async_remote_copy(
-            src_ref=rsend.at[c, way, pair],
-            dst_ref=rrecv.at[c, way, pair],
-            send_sem=hs1.at[c, way, pair],
-            recv_sem=hr1.at[c, way, pair],
+            src_ref=rsend.at[c, way],
+            dst_ref=rrecv.at[c, way],
+            send_sem=hs1.at[c, way],
+            recv_sem=hr1.at[c, way],
             device_id=((up, down)[way], me),
             device_id_type=MESH,
         )
@@ -380,11 +382,6 @@
                 nodes = jnp.concatenate(nodes, axis=0) if count > 1 else nodes[0]
                 packed.append(pick(nodes, tables[t + k]))
         return packed[0] + packed[1], packed[2] + packed[3]
-
-    def send_r_edges(c, pair):
-        for way, got in enumerate(pack_edges(res, c, pair, 1)):
-            rsend[c, way, pair] = got
-            r_halo(c, way, pair).start()
 
     def send_q_edges(c):
         for way, got in enumerate(pack_edges(qv, c, 0, AH)):
@@ -451,7 +448,7 @@
 
     def arrive_second(c, ah):
         groups = [fbuf[g % HALVES, c, g // HALVES, ah] for g in range(GROUPS)]
-        for k, line in enumerate(block_transpose(groups)):
+        for k, line in enumerate(block_transpose(groups, True)):
             res[ah * 2 * N + k, sys_rows(c), :] = line
 
     def dot_rows(first, k, count):
@@ -460,7 +457,6 @@
     def begin(c):
         def arrive(ah, carry):
             arrive_second(c, ah)
-            send_r_edges(c, ah)
             return carry
 
         def arrive_pair(k, carry):
@@ -470,18 +466,18 @@
             return lax.fori_loop(2 * k, 2 * k + 2, arrive, carry)
 
         lax.fori_loop(0, 2, arrive_pair, 0)
+        for way, got in enumerate(pack_edges(res, c, 0, AH)):
+            rsend[c, way] = got.reshape(AH, ZL, ED)
         take_faces(res, c)
+        for way in (0, 1):
+            r_halo(c, way).start()
         apply_local(res, qv, c, (0,))
         send_q_edges(c)
         apply_local(res, qv, c, (1, 2, 3))
 
     def end(c):
-        def wait_r(k, carry):
-            for way in (0, 1):
-                r_halo(c, way, k).wait_recv()
-            return carry
-
-        lax.fori_loop(0, AH, wait_r, 0)
+        for way in (0, 1):
+            r_halo(c, way).wait_recv()
         take_edges(rrecv, c)
         add_edges(qv, c)
         take_faces(qv, c)
@@ -582,8 +578,7 @@
 
     def drain3(c, carry):
         for way in (0, 1):
-            for pair in range(AH):
-                r_halo(c, way, pair).wait_send()
+            r_halo(c, way).wait_send()
             q_halo(c, way).wait_send()
         return carry
 
@@ -682,8 +677,8 @@
             dma((HALVES, AH, NP - 1)),
             dma((HALVES, 3, 2, NP - 1)),
             dma((HALVES, 3, 2, NP - 1)),
-            dma((3, 2, AH)),
-            dma((3, 2, AH)),
+            dma((3, 2)),
+            dma((3, 2)),
             dma((3, 2)),
             dma((3, 2)),
             dma((NE - 1,)),

time: 67.2 us -> 64.8 us (0.964)
  Pallas kernels: 65.7 us -> 63.7 us
    pallas_call x1, Pallas kernels: 63.8 us -> 61.8 us  [on_device(): pl.pallas_call(kernel, out_shape=(field, field, field, jax.ShapeDtypeStru...]
where the time goes in v5:
time: 64.8 us; the launch traced here: 64.3 us
  Pallas kernels  63.7 us (98%)
    pallas_call x1, Pallas kernels, on_device(): pl.pallas_call(kernel, out_shape=(field, field, field, jax.ShapeDtypeStru...  61.8 us
    pallas_call x1, Pallas kernels, on_device(): pl.pallas_call(finish_kernel, out_shape=(flat, flat), in_specs=[vmem] * 4...  1.83 us

profile of v5, /device:TPU:2, one launch (start us, length us, event | category | flops | bytes accessed | tf_op | source)
XLA Modules:
  0.0 64.3 jit_solution(9411146844754387156)
XLA Ops:
  0.6 61.8 %exchange_and_apply.1 = (f32[64,48,128]{2,1,0:T(8,128)S(1)}, f32[64,48,128]{2,1,0:T(8,128)S(1)}, f32[64,48,128]{2,1,0:T(8,128)S(1)}, f32[2,48,128]{2,1,0:T(8,128)S(1)}) custom-call(f32[48,64,128]{2,1,0:T(8,128)} %bitcast.3, f32[2,128]{1,0:T(2,128)} %scale_in.1, s32[1,128]{1,0:T(1,128)} %ids_in.1, f32[40,128]{1,0:T(8,128)} %constant.4.clone.rows_in, ...), custom_call_target="tpu_custom_call" | custom-call | tf_op jit(solution)/shard_map/exchange_and_apply/pallas_call | solution.py:646
  62.5 1.8 %finish.1 = (f32[6,512,128]{2,1,0:T(8,128)}, f32[6,512,128]{2,1,0:T(8,128)}) custom-call(f32[64,48,128]{2,1,0:T(8,128)S(1)} %get-tuple-element.8.r, f32[64,48,128]{2,1,0:T(8,128)S(1)} %get-tuple-element.9.q, f32[64,48,128]{2,1,0:T(8,128)S(1)} %get-tuple-element.10.p, f32[2,48,128]{2,1,0:T(8,128)S(1)} %get-tuple-element.11.coef), custom_call_target="tpu_custom_call" | custom-call | tf_op jit(solution)/shard_map/finish/pallas_call | solution.py:694

commit v6 on v5

--- a/solution.py
+++ b/solution.py
@@ -195,6 +195,59 @@
     for t in elem_peers:
         pl.semaphore_signal(barrier, inc=1, device_id=(t, me), device_id_type=MESH)
 
+    def copy1(half, ah, i):
+        t = plane_peers[i]
+        return pltpu.make_async_remote_copy(
+            src_ref=xsend.at[half, ah, t],
+            dst_ref=xbuf.at[half, ah, :, pl.ds(pl.multiple_of(me * ZL, ZL), ZL), :],
+            send_sem=s1.at[half, ah, i],
+            recv_sem=r1.at[half, ah, i],
+            device_id=(e, t),
+            device_id_type=MESH,
+        )
+
+    def copy2(half, c, k, i):
+        t = plane_peers[i]
+        return pltpu.make_async_remote_copy(
+            src_ref=fsend.at[half, c, pl.ds(2 * k, 2), pl.ds(pl.multiple_of(t * ZL, ZL), ZL), :],
+            dst_ref=fbuf.at[half, c, me, pl.ds(2 * k, 2)],
+            send_sem=s2.at[half, c, k, i],
+            recv_sem=r2.at[half, c, k, i],
+            device_id=(e, t),
+            device_id_type=MESH,
+        )
+
+    def pack_first(ah):
+        for c in range(3):
+            for z8 in range(ZL // 8):
+                nodes = pl.ds(pl.multiple_of(ah * 2 * N, 2 * N), 2 * N)
+                tile = jnp.swapaxes(vin[pl.ds(c * ZL + z8 * 8, 8), nodes, :], 0, 1)
+                for g, row in enumerate(block_transpose([tile[k] for k in range(2 * N)])):
+                    xsend[g % HALVES, ah, g // HALVES, c, pl.ds(z8 * 8, 8), :] = row
+
+    def send_first(half, ah):
+        for i in range(NP - 1):
+            copy1(half, ah, i).start()
+        mine = pl.ds(pl.multiple_of(me * ZL, ZL), ZL)
+        xbuf[half, ah, :, mine, :] = xsend[half, ah, me]
+
+    loads[0].wait()
+    pack_first(0)
+    pl.semaphore_wait(barrier, NP - 1 + NE - 1)
+    send_first(0, 0)
+
+    def first(ah, carry):
+        pack_first(ah)
+        send_first(0, ah)
+        return carry
+
+    def first_rest(ah, carry):
+        send_first(1, ah)
+        return carry
+
+    lax.fori_loop(1, AH, first, 0)
+    lax.fori_loop(0, AH, first_rest, 0)
+
     for load in loads[1:]:
         load.wait()
 
@@ -218,59 +271,6 @@
         part_geo[half, 0:1, :] = g_circ * g_radial
         part_geo[half, 1:2, :] = g_circ
         part_geo[half, 2:3, :] = g_radial * ctab[ROW_B : ROW_B + 1, :]
-
-    def copy1(half, ah, i):
-        t = plane_peers[i]
-        return pltpu.make_async_remote_copy(
-            src_ref=xsend.at[half, ah, t],
-            dst_ref=xbuf.at[half, ah, :, pl.ds(pl.multiple_of(me * ZL, ZL), ZL), :],
-            send_sem=s1.at[half, ah, i],
-            recv_sem=r1.at[half, ah, i],
-            device_id=(e, t),
-            device_id_type=MESH,
-        )
-
-    def copy2(half, c, k, i):
-        t = plane_peers[i]
-        return pltpu.make_async_remote_copy(
-            src_ref=fsend.at[half, c, pl.ds(2 * k, 2), pl.ds(pl.multiple_of(t * ZL, ZL), ZL), :],
-            dst_ref=fbuf.at[half, c, me, pl.ds(2 * k, 2)],
-            send_sem=s2.at[half, c, k, i],
-            recv_sem=r2.at[half, c, k, i],
-            device_id=(e, t),
-            device_id_type=MESH,
-        )
-
-    def pack_first(ah):
-        for c in range(3):
-            for z8 in range(ZL // 8):
-                nodes = pl.ds(pl.multiple_of(ah * 2 * N, 2 * N), 2 * N)
-                tile = jnp.swapaxes(vin[pl.ds(c * ZL + z8 * 8, 8), nodes, :], 0, 1)
-                for g, row in enumerate(block_transpose([tile[k] for k in range(2 * N)])):
-                    xsend[g % HALVES, ah, g // HALVES, c, pl.ds(z8 * 8, 8), :] = row
-
-    def send_first(half, ah):
-        for i in range(NP - 1):
-            copy1(half, ah, i).start()
-        mine = pl.ds(pl.multiple_of(me * ZL, ZL), ZL)
-        xbuf[half, ah, :, mine, :] = xsend[half, ah, me]
-
-    loads[0].wait()
-    pack_first(0)
-    pl.semaphore_wait(barrier, NP - 1 + NE - 1)
-    send_first(0, 0)
-
-    def first(ah, carry):
-        pack_first(ah)
-        send_first(0, ah)
-        return carry
-
-    def first_rest(ah, carry):
-        send_first(1, ah)
-        return carry
-
-    lax.fori_loop(1, AH, first, 0)
-    lax.fori_loop(0, AH, first_rest, 0)
 
     acc[...] = jnp.zeros_like(acc)
     dots[...] = jnp.zeros_like(dots)
@@ -350,12 +350,12 @@
     def sys_rows(c):
         return pl.ds(pl.multiple_of(c * ZL, ZL), ZL)
 
-    def r_halo(c, way):
+    def r_halo(c, way, k):
         return pltpu.make_async_remote_copy(
-            src_ref=rsend.at[c, way],
-            dst_ref=rrecv.at[c, way],
-            send_sem=hs1.at[c, way],
-            recv_sem=hr1.at[c, way],
+            src_ref=rsend.at[c, way, pl.ds(2 * k, 2)],
+            dst_ref=rrecv.at[c, way, pl.ds(2 * k, 2)],
+            send_sem=hs1.at[c, way, k],
+            recv_sem=hr1.at[c, way, k],
             device_id=((up, down)[way], me),
             device_id_type=MESH,
         )
@@ -459,25 +459,25 @@
             arrive_second(c, ah)
             return carry
 
-        def arrive_pair(k, carry):
+        for k in (0, 1):
             for half in range(HALVES):
                 for i in range(NP - 1):
                     copy2(half, c, k, i).wait_recv()
-            return lax.fori_loop(2 * k, 2 * k + 2, arrive, carry)
-
-        lax.fori_loop(0, 2, arrive_pair, 0)
-        for way, got in enumerate(pack_edges(res, c, 0, AH)):
-            rsend[c, way] = got.reshape(AH, ZL, ED)
-        take_faces(res, c)
-        for way in (0, 1):
-            r_halo(c, way).start()
+            lax.fori_loop(2 * k, 2 * k + 2, arrive, 0)
+            for way, got in enumerate(pack_edges(res, c, 2 * k, 2)):
+                rsend[c, way, pl.ds(2 * k, 2)] = got.reshape(2, ZL, ED)
+            if k == 1:
+                take_faces(res, c)
+            for way in (0, 1):
+                r_halo(c, way, k).start()
         apply_local(res, qv, c, (0,))
         send_q_edges(c)
         apply_local(res, qv, c, (1, 2, 3))
 
     def end(c):
         for way in (0, 1):
-            r_halo(c, way).wait_recv()
+            for k in (0, 1):
+                r_halo(c, way, k).wait_recv()
         take_edges(rrecv, c)
         add_edges(qv, c)
         take_faces(qv, c)
@@ -519,8 +519,10 @@
         end(c)
         return carry
 
-    lax.fori_loop(0, 3, begin_all, 0)
-    lax.fori_loop(0, 3, end_all, 0)
+    lax.fori_loop(0, 2, begin_all, 0)
+    end(0)
+    begin(2)
+    lax.fori_loop(1, 3, end_all, 0)
 
     one_rows = jnp.ones((8, ED), F32)
     for k in (0, 1):
@@ -578,7 +580,8 @@
 
     def drain3(c, carry):
         for way in (0, 1):
-            r_halo(c, way).wait_send()
+            for k in (0, 1):
+                r_halo(c, way, k).wait_send()
             q_halo(c, way).wait_send()
         return carry
 
@@ -677,8 +680,8 @@
             dma((HALVES, AH, NP - 1)),
             dma((HALVES, 3, 2, NP - 1)),
             dma((HALVES, 3, 2, NP - 1)),
-            dma((3, 2)),
-            dma((3, 2)),
+            dma((3, 2, 2)),
+            dma((3, 2, 2)),
             dma((3, 2)),
             dma((3, 2)),
             dma((NE - 1,)),

time: 64.8 us -> 66.3 us (1.023)
  Pallas kernels: 63.7 us -> 65.2 us
    pallas_call x1, Pallas kernels: 61.8 us -> 63.4 us  [on_device(): pl.pallas_call(kernel, out_shape=(field, field, field, jax.ShapeDtypeStru...]
where the time goes in v6:
time: 66.3 us; the launch traced here: 65.8 us
  Pallas kernels  65.2 us (98%)
    pallas_call x1, Pallas kernels, on_device(): pl.pallas_call(kernel, out_shape=(field, field, field, jax.ShapeDtypeStru...  63.4 us
    pallas_call x1, Pallas kernels, on_device(): pl.pallas_call(finish_kernel, out_shape=(flat, flat), in_specs=[vmem] * 4...  1.83 us

profile of v6, /device:TPU:2, one launch (start us, length us, event | category | flops | bytes accessed | tf_op | source)
XLA Modules:
  0.0 65.8 jit_solution(15841213391995882563)
XLA Ops:
  0.6 63.4 %exchange_and_apply.1 = (f32[64,48,128]{2,1,0:T(8,128)S(1)}, f32[64,48,128]{2,1,0:T(8,128)S(1)}, f32[64,48,128]{2,1,0:T(8,128)S(1)}, f32[2,48,128]{2,1,0:T(8,128)S(1)}) custom-call(f32[48,64,128]{2,1,0:T(8,128)} %bitcast.3, f32[2,128]{1,0:T(2,128)} %scale_in.1, s32[1,128]{1,0:T(1,128)} %ids_in.1, f32[40,128]{1,0:T(8,128)} %constant.4.clone.rows_in, ...), custom_call_target="tpu_custom_call" | custom-call | tf_op jit(solution)/shard_map/exchange_and_apply/pallas_call | solution.py:649
  64.0 1.8 %finish.1 = (f32[6,512,128]{2,1,0:T(8,128)}, f32[6,512,128]{2,1,0:T(8,128)}) custom-call(f32[64,48,128]{2,1,0:T(8,128)S(1)} %get-tuple-element.8.r, f32[64,48,128]{2,1,0:T(8,128)S(1)} %get-tuple-element.9.q, f32[64,48,128]{2,1,0:T(8,128)S(1)} %get-tuple-element.10.p, f32[2,48,128]{2,1,0:T(8,128)S(1)} %get-tuple-element.11.coef), custom_call_target="tpu_custom_call" | custom-call | tf_op jit(solution)/shard_map/finish/pallas_call | solution.py:697

commit v7 on v6

--- a/solution.py
+++ b/solution.py
@@ -27,6 +27,7 @@
 NX = 4
 NZ = 8
 NE = NX * NZ
+EARLY = 5
 PEN = 8.0
 ROW_SAME, ROW_SWAP, ROW_AB, ROW_B = 0, AH * AH, 2 * AH * AH, 2 * AH * AH + AH
 ROWS = 40
@@ -335,8 +336,11 @@
                 low = jnp.concatenate([a_low, bbuf[half, ah, 1, c]], axis=0)
                 out = dot(f_high, high) + dot(f_high, low) + dot(f_low, high)
                 fsend[half, c, ah] = pltpu.roll(out, EG * (HALVES * me + half), 1)
-            for i in range(NP - 1):
-                copy2(half, c, k, i).start()
+            @pl.when((half == 0) | (step < EARLY))
+            def _():
+                for i in range(NP - 1):
+                    copy2(half, c, k, i).start()
+
             mine = pl.ds(pl.multiple_of(me * ZL, ZL), ZL)
             fbuf[half, c, me, pl.ds(2 * k, 2)] = fsend[half, c, pl.ds(2 * k, 2), mine, :]
             return carry
@@ -513,16 +517,21 @@
 
     def begin_all(c, carry):
         begin(c)
+
+        @pl.when(c == 0)
+        def _():
+            for step in range(EARLY, 6):
+                for i in range(NP - 1):
+                    copy2(1, step // 2, step % 2, i).start()
+
         return carry
 
     def end_all(c, carry):
         end(c)
         return carry
 
-    lax.fori_loop(0, 2, begin_all, 0)
-    end(0)
-    begin(2)
-    lax.fori_loop(1, 3, end_all, 0)
+    lax.fori_loop(0, 3, begin_all, 0)
+    lax.fori_loop(0, 3, end_all, 0)
 
     one_rows = jnp.ones((8, ED), F32)
     for k in (0, 1):

time: 66.3 us -> 64.4 us (0.971)
  Pallas kernels: 65.2 us -> 63.4 us
    pallas_call x1, Pallas kernels: 63.4 us -> 61.6 us  [on_device(): pl.pallas_call(kernel, out_shape=(field, field, field, jax.ShapeDtypeStru...]
where the time goes in v7:
time: 64.4 us; the launch traced here: 64 us
  Pallas kernels  63.4 us (98%)
    pallas_call x1, Pallas kernels, on_device(): pl.pallas_call(kernel, out_shape=(field, field, field, jax.ShapeDtypeStru...  61.6 us
    pallas_call x1, Pallas kernels, on_device(): pl.pallas_call(finish_kernel, out_shape=(flat, flat), in_specs=[vmem] * 4...  1.83 us

profile of v7, /device:TPU:2, one launch (start us, length us, event | category | flops | bytes accessed | tf_op | source)
XLA Modules:
  0.0 64.0 jit_solution(6716504970235123212)
XLA Ops:
  0.6 61.6 %exchange_and_apply.1 = (f32[64,48,128]{2,1,0:T(8,128)S(1)}, f32[64,48,128]{2,1,0:T(8,128)S(1)}, f32[64,48,128]{2,1,0:T(8,128)S(1)}, f32[2,48,128]{2,1,0:T(8,128)S(1)}) custom-call(f32[48,64,128]{2,1,0:T(8,128)} %bitcast.3, f32[2,128]{1,0:T(2,128)} %scale_in.1, s32[1,128]{1,0:T(1,128)} %ids_in.1, f32[40,128]{1,0:T(8,128)} %constant.4.clone.rows_in, ...), custom_call_target="tpu_custom_call" | custom-call | tf_op jit(solution)/shard_map/exchange_and_apply/pallas_call | solution.py:658
  62.2 1.8 %finish.1 = (f32[6,512,128]{2,1,0:T(8,128)}, f32[6,512,128]{2,1,0:T(8,128)}) custom-call(f32[64,48,128]{2,1,0:T(8,128)S(1)} %get-tuple-element.8.r, f32[64,48,128]{2,1,0:T(8,128)S(1)} %get-tuple-element.9.q, f32[64,48,128]{2,1,0:T(8,128)S(1)} %get-tuple-element.10.p, f32[2,48,128]{2,1,0:T(8,128)S(1)} %get-tuple-element.11.coef), custom_call_target="tpu_custom_call" | custom-call | tf_op jit(solution)/shard_map/finish/pallas_call | solution.py:706

commit v8 on v7

--- a/solution.py
+++ b/solution.py
@@ -186,8 +186,16 @@
     ]
     up, down = lax.rem(e + 1, NE), lax.rem(e + NE - 1, NE)
 
-    pairs = ((vel, vin), (scale_in, scale), (ids_in, ids), (rows_in, ctab), (mats_in, mats))
-    loads = [pltpu.make_async_copy(src, dst, in_sem.at[i]) for i, (src, dst) in enumerate(pairs)]
+    def load_nodes(ah):
+        nodes = pl.ds(pl.multiple_of(ah * 2 * N, 2 * N), 2 * N)
+        return pltpu.make_async_copy(vel.at[:, nodes, :], vin.at[:, nodes, :], in_sem.at[ah])
+
+    for ah in range(AH):
+        load_nodes(ah).start()
+    pairs = ((scale_in, scale), (ids_in, ids), (rows_in, ctab), (mats_in, mats))
+    loads = [
+        pltpu.make_async_copy(src, dst, in_sem.at[AH + i]) for i, (src, dst) in enumerate(pairs)
+    ]
     for load in loads:
         load.start()
     barrier = pltpu.get_barrier_semaphore()
@@ -219,6 +227,7 @@
         )
 
     def pack_first(ah):
+        load_nodes(ah).wait()
         for c in range(3):
             for z8 in range(ZL // 8):
                 nodes = pl.ds(pl.multiple_of(ah * 2 * N, 2 * N), 2 * N)
@@ -232,7 +241,6 @@
         mine = pl.ds(pl.multiple_of(me * ZL, ZL), ZL)
         xbuf[half, ah, :, mine, :] = xsend[half, ah, me]
 
-    loads[0].wait()
     pack_first(0)
     pl.semaphore_wait(barrier, NP - 1 + NE - 1)
     send_first(0, 0)
@@ -249,7 +257,7 @@
     lax.fori_loop(1, AH, first, 0)
     lax.fori_loop(0, AH, first_rest, 0)
 
-    for load in loads[1:]:
+    for load in loads:
         load.wait()
 
     lid = ids[...] & (ED - 1)
@@ -556,6 +564,32 @@
 
     for i in range(NE - 1):
         spread(i).start()
+
+    def drain(ah, carry):
+        for half in range(HALVES):
+            for i in range(NP - 1):
+                copy1(half, ah, i).wait_send()
+        return carry
+
+    def drain2(step, carry):
+        for half in range(HALVES):
+            for i in range(NP - 1):
+                copy2(half, step // 2, lax.rem(step, 2), i).wait_send()
+        return carry
+
+    def drain3(c, carry):
+        for way in (0, 1):
+            for k in (0, 1):
+                r_halo(c, way, k).wait_send()
+            q_halo(c, way).wait_send()
+        return carry
+
+    lax.fori_loop(0, AH, drain, 0)
+    lax.fori_loop(0, 6, drain2, 0)
+    lax.fori_loop(0, 3, drain3, 0)
+    for i in range(NE - 1):
+        spread(i).wait_send()
+
     for i in range(NE - 1):
         spread(i).wait_recv()
     part = jnp.sum(rbuf[...], axis=0)
@@ -574,31 +608,6 @@
     both = jnp.transpose(jnp.concatenate([both] + [jnp.zeros((8, ED), F32)] * 15, axis=0))
     coef_out[0] = jnp.broadcast_to(both[0:SYS, 0:1], (SYS, ED))
     coef_out[1] = jnp.broadcast_to(both[0:SYS, 1:2], (SYS, ED))
-
-    def drain(ah, carry):
-        for half in range(HALVES):
-            for i in range(NP - 1):
-                copy1(half, ah, i).wait_send()
-        return carry
-
-    def drain2(step, carry):
-        for half in range(HALVES):
-            for i in range(NP - 1):
-                copy2(half, step // 2, lax.rem(step, 2), i).wait_send()
-        return carry
-
-    def drain3(c, carry):
-        for way in (0, 1):
-            for k in (0, 1):
-                r_halo(c, way, k).wait_send()
-            q_halo(c, way).wait_send()
-        return carry
-
-    lax.fori_loop(0, AH, drain, 0)
-    lax.fori_loop(0, 6, drain2, 0)
-    lax.fori_loop(0, 3, drain3, 0)
-    for i in range(NE - 1):
-        spread(i).wait_send()
 
 
 def finish_kernel(r, q, p, coef, x_out, r_out, xs, rs, sem):
@@ -684,7 +693,7 @@
             pltpu.VMEM((3, 2, AH, ZL, ED), F32),
             pltpu.VMEM((2, ED, ED), F32),
             pltpu.VMEM((NE, 2, ED), F32),
-            dma((5,)),
+            dma((AH + 4,)),
             dma((HALVES, AH, NP - 1)),
             dma((HALVES, AH, NP - 1)),
             dma((HALVES, 3, 2, NP - 1)),

time: 64.4 us -> 64.1 us (level)
  no operation moved by 1% of the time
where the time goes in v8:
time: 64.1 us; the launch traced here: 63.8 us
  Pallas kernels  63.1 us (98%)
    pallas_call x1, Pallas kernels, on_device(): pl.pallas_call(kernel, out_shape=(field, field, field, jax.ShapeDtypeStru...  61.3 us
    pallas_call x1, Pallas kernels, on_device(): pl.pallas_call(finish_kernel, out_shape=(flat, flat), in_specs=[vmem] * 4...  1.83 us

profile of v8, /device:TPU:2, one launch (start us, length us, event | category | flops | bytes accessed | tf_op | source)
XLA Modules:
  0.0 63.8 jit_solution(17228010367600714751)
XLA Ops:
  0.6 61.3 %exchange_and_apply.1 = (f32[64,48,128]{2,1,0:T(8,128)S(1)}, f32[64,48,128]{2,1,0:T(8,128)S(1)}, f32[64,48,128]{2,1,0:T(8,128)S(1)}, f32[2,48,128]{2,1,0:T(8,128)S(1)}) custom-call(f32[48,64,128]{2,1,0:T(8,128)} %bitcast.3, f32[2,128]{1,0:T(2,128)} %scale_in.1, s32[1,128]{1,0:T(1,128)} %ids_in.1, f32[40,128]{1,0:T(8,128)} %constant.4.clone.rows_in, ...), custom_call_target="tpu_custom_call" | custom-call | tf_op jit(solution)/shard_map/exchange_and_apply/pallas_call | solution.py:667
  61.9 1.8 %finish.1 = (f32[6,512,128]{2,1,0:T(8,128)}, f32[6,512,128]{2,1,0:T(8,128)}) custom-call(f32[64,48,128]{2,1,0:T(8,128)S(1)} %get-tuple-element.8.r, f32[64,48,128]{2,1,0:T(8,128)S(1)} %get-tuple-element.9.q, f32[64,48,128]{2,1,0:T(8,128)S(1)} %get-tuple-element.10.p, f32[2,48,128]{2,1,0:T(8,128)S(1)} %get-tuple-element.11.coef), custom_call_target="tpu_custom_call" | custom-call | tf_op jit(solution)/shard_map/finish/pallas_call | solution.py:715

commit v9 on v8

--- a/solution.py
+++ b/solution.py
@@ -186,6 +186,10 @@
     ]
     up, down = lax.rem(e + 1, NE), lax.rem(e + NE - 1, NE)
 
+    barrier = pltpu.get_barrier_semaphore()
+    for t in plane_peers:
+        pl.semaphore_signal(barrier, inc=1, device_id=(e, t), device_id_type=MESH)
+
     def load_nodes(ah):
         nodes = pl.ds(pl.multiple_of(ah * 2 * N, 2 * N), 2 * N)
         return pltpu.make_async_copy(vel.at[:, nodes, :], vin.at[:, nodes, :], in_sem.at[ah])
@@ -198,9 +202,6 @@
     ]
     for load in loads:
         load.start()
-    barrier = pltpu.get_barrier_semaphore()
-    for t in plane_peers:
-        pl.semaphore_signal(barrier, inc=1, device_id=(e, t), device_id_type=MESH)
     for t in elem_peers:
         pl.semaphore_signal(barrier, inc=1, device_id=(t, me), device_id_type=MESH)
 
@@ -541,15 +542,15 @@
     lax.fori_loop(0, 3, begin_all, 0)
     lax.fori_loop(0, 3, end_all, 0)
 
-    one_rows = jnp.ones((8, ED), F32)
+    one_rows = jnp.ones((8, ED), BF16)
     for k in (0, 1):
-        summed = lax.dot_general(
-            one_rows,
-            dots[k],
-            (((1,), (1,)), ((), ())),
-            precision=lax.Precision.HIGHEST,
-            preferred_element_type=F32,
-        )
+        high, rest = split(dots[k])
+        low = dots[k] - high.astype(F32) - rest.astype(F32)
+        summed = jnp.zeros((8, ED), F32)
+        for term in (low.astype(BF16), rest, high):
+            summed = summed + lax.dot_general(
+                one_rows, term, (((1,), (1,)), ((), ())), preferred_element_type=F32
+            )
         rbuf[0, k : k + 1, :] = summed[0:1, :]
 
     def spread(i):

time: 64.1 us -> 64 us (level)
  no operation moved by 1% of the time
where the time goes in v9:
time: 64 us; the launch traced here: 63.6 us
  Pallas kernels  63 us (98%)
  between operations  0.64 us (1%)
    pallas_call x1, Pallas kernels, on_device(): pl.pallas_call(kernel, out_shape=(field, field, field, jax.ShapeDtypeStru...  61.2 us
    pallas_call x1, Pallas kernels, on_device(): pl.pallas_call(finish_kernel, out_shape=(flat, flat), in_specs=[vmem] * 4...  1.83 us

profile of v9, /device:TPU:2, one launch (start us, length us, event | category | flops | bytes accessed | tf_op | source)
XLA Modules:
  0.0 63.6 jit_solution(2848908599494208298)
XLA Ops:
  0.6 61.2 %exchange_and_apply.1 = (f32[64,48,128]{2,1,0:T(8,128)S(1)}, f32[64,48,128]{2,1,0:T(8,128)S(1)}, f32[64,48,128]{2,1,0:T(8,128)S(1)}, f32[2,48,128]{2,1,0:T(8,128)S(1)}) custom-call(f32[48,64,128]{2,1,0:T(8,128)} %bitcast.3, f32[2,128]{1,0:T(2,128)} %scale_in.1, s32[1,128]{1,0:T(1,128)} %ids_in.1, f32[40,128]{1,0:T(8,128)} %constant.4.clone.rows_in, ...), custom_call_target="tpu_custom_call" | custom-call | tf_op jit(solution)/shard_map/exchange_and_apply/pallas_call | solution.py:668
  61.8 1.8 %finish.1 = (f32[6,512,128]{2,1,0:T(8,128)}, f32[6,512,128]{2,1,0:T(8,128)}) custom-call(f32[64,48,128]{2,1,0:T(8,128)S(1)} %get-tuple-element.8.r, f32[64,48,128]{2,1,0:T(8,128)S(1)} %get-tuple-element.9.q, f32[64,48,128]{2,1,0:T(8,128)S(1)} %get-tuple-element.10.p, f32[2,48,128]{2,1,0:T(8,128)S(1)} %get-tuple-element.11.coef), custom_call_target="tpu_custom_call" | custom-call | tf_op jit(solution)/shard_map/finish/pallas_call | solution.py:716
